TPU v7x, 256 devices: a whole 4x4x8 slice. The times are simulated.
256 devices in a mesh: dp: 32 (over z, y), tensor: 8 (over x, core).
Axes of the slice: x: 4, y: 4, z: 8, core: 2. Of those that a mesh axis runs over, the one named last changes fastest.
Arguments:
- hidden_in: bfloat16 [65536, 14336], P('dp', 'tensor'), may hold values from -6 to 6
- out_grad: bfloat16 [65536, 4096], P('dp', 'tensor'), may hold values from -6 to 6
- proj_in: bfloat16 [14336, 64], P('tensor'), may hold values from -0.046875 to 0.046875
- proj_out: bfloat16 [4096, 64], P('tensor'), may hold values from -0.09375 to 0.09375
- token_mask: int32 [65536], P('dp'), may hold values 0 or 1
- cand_ids: int32 [32], P('dp'), may hold values from 0 to 1023
- queries: bfloat16 [1024, 4096], P('tensor', 'dp'), may hold values from -6 to 6
Outputs:
- scores: float32 [32, 1024], P('dp', 'tensor')
All inputs are finite; a program needn't handle non-finite values. No bound on the sum of `token_mask` on one device may be relied on, other than what follows from the above.
Results may differ from a plain program's by a relative error of at most 0.0029.
Values may be sent and summed in bfloat16 or wider, within the bound.
No kernel may reach another device: no remote copies, remote signals or barrier semaphores. Data moves between devices by JAX's collectives and lax.ppermute only.
A program may use at most 64 MiB of HBM per device.

v0:
```python
import functools

import jax
import jax.numpy as jnp
from jax import lax
from jax.experimental import pallas as pl
from jax.experimental.pallas import tpu as pltpu
from jax.sharding import PartitionSpec as P

BLOCK = 256
OUTER_FLOPS = 4 << 30
PROJECT_VMEM = 16 << 20
SMALL_VMEM = 8 << 20
ROWS = 4
NO_COST = pl.CostEstimate(flops=0, bytes_accessed=0, transcendentals=0)
HIGHEST = lax.Precision.HIGHEST


def nt_dot(a, b, precision=None):
    return lax.dot_general(
        a, b, (((1,), (1,)), ((), ())), preferred_element_type=jnp.float32, precision=precision
    )


def project_block(hidden, grad, w):
    width = hidden.shape[1]
    return nt_dot(hidden, w[:, :width]) + nt_dot(grad, w[:, width:])


def theirs_kernel(n, place_ref, hidden_ref, grad_ref, pin_ref, pout_ref, *refs):
    outs, (own_hidden, own_grad, w_ref, hidden, grad, sem, w_sem) = refs[:n], refs[n:]
    rank, width = pin_ref.shape
    depth = pout_ref.shape[1]
    weights = [
        pltpu.make_async_copy(pin_ref, w_ref.at[pl.ds(0, rank), pl.ds(0, width)], w_sem.at[0]),
        pltpu.make_async_copy(pout_ref, w_ref.at[pl.ds(rank, rank), pl.ds(width, depth)], w_sem.at[1]),
    ]
    copies = []
    for j, (half, buffers) in enumerate(((1 - place_ref[0], (hidden, grad)), (place_ref[0], (own_hidden, own_grad)))):
        for k in range(n):
            first = (half * n + jnp.bitwise_xor(place_ref[1], k)) * BLOCK
            rows = pl.ds(pl.multiple_of(first, BLOCK), BLOCK)
            for i, (source, buffer) in enumerate(zip((hidden_ref, grad_ref), buffers)):
                copies.append(
                    pltpu.make_async_copy(source.at[rows, :], buffer.at[pl.ds(k * BLOCK, BLOCK), :], sem.at[j, k, i])
                )
    for copy in weights + copies[: 2 * n]:
        copy.start()
    w_ref[rank:, :width] = jnp.zeros((rank, width), w_ref.dtype)
    w_ref[:rank, width:] = jnp.zeros((rank, depth), w_ref.dtype)
    for copy in weights:
        copy.wait()
    for copy in copies[2 * n :]:
        copy.start()
    for copy in copies[: 2 * n]:
        copy.wait()
    for k in range(n):
        rows = pl.ds(k * BLOCK, BLOCK)
        outs[k][...] = project_block(hidden[rows, :], grad[rows, :], w_ref)
    for copy in copies[2 * n :]:
        copy.wait()


def project_theirs(place, hidden, grad, pin_t, pout_t):
    rank, width = pin_t.shape
    depth = pout_t.shape[1]
    half = hidden.shape[0] // 2
    n = half // BLOCK
    vmem = pl.BlockSpec(memory_space=pltpu.VMEM)
    hbm = pl.BlockSpec(memory_space=pltpu.HBM)
    held = [pltpu.with_memory_space_constraint(x, pltpu.HBM) for x in (hidden, grad, pin_t, pout_t)]
    outs = pl.pallas_call(
        functools.partial(theirs_kernel, n),
        out_shape=[jax.ShapeDtypeStruct((BLOCK, 2 * rank), jnp.float32)] * n
        + [
            pltpu.VMEM((half, width), hidden.dtype),
            pltpu.VMEM((half, depth), grad.dtype),
            pltpu.VMEM((2 * rank, width + depth), pin_t.dtype),
        ],
        in_specs=[pl.BlockSpec(memory_space=pltpu.SMEM)] + [hbm] * 4,
        out_specs=[vmem] * (n + 3),
        scratch_shapes=[
            pltpu.VMEM((half, width), hidden.dtype),
            pltpu.VMEM((half, depth), grad.dtype),
            pltpu.SemaphoreType.DMA((2, n, 2)),
            pltpu.SemaphoreType.DMA((2,)),
        ],
        compiler_params=pltpu.CompilerParams(vmem_limit_bytes=PROJECT_VMEM),
        cost_estimate=NO_COST,
        name="project_theirs",
    )(place, *held)
    return outs[:n], outs[n:]


def mine_kernel(hidden_ref, grad_ref, w_ref, *outs):
    for k, out in enumerate(outs):
        rows = pl.ds(k * BLOCK, BLOCK)
        out[...] = project_block(hidden_ref[rows, :], grad_ref[rows, :], w_ref)


def project_mine(hidden, grad, w):
    n = hidden.shape[0] // BLOCK
    vmem = pl.BlockSpec(memory_space=pltpu.VMEM)
    held = [pltpu.with_memory_space_constraint(x, pltpu.VMEM) for x in (hidden, grad, w)]
    return pl.pallas_call(
        mine_kernel,
        out_shape=[jax.ShapeDtypeStruct((BLOCK, w.shape[0]), jnp.float32)] * n,
        in_specs=[vmem] * 3,
        out_specs=[vmem] * n,
        compiler_params=pltpu.CompilerParams(vmem_limit_bytes=SMALL_VMEM),
        cost_estimate=NO_COST,
        name="project_mine",
    )(*held)


def pair_kernel(*refs):
    n = len(refs) // 3
    for a_ref, b_ref, out_ref in zip(refs[:n], refs[n : 2 * n], refs[2 * n :]):
        out_ref[...] = a_ref[...] + b_ref[...]


def pair_sum(a, b):
    vmem = pl.BlockSpec(memory_space=pltpu.VMEM)
    return pl.pallas_call(
        pair_kernel,
        out_shape=[jax.ShapeDtypeStruct(x.shape, x.dtype) for x in a],
        in_specs=[vmem] * (2 * len(a)),
        out_specs=[vmem] * len(a),
        compiler_params=pltpu.CompilerParams(vmem_limit_bytes=SMALL_VMEM),
        cost_estimate=NO_COST,
        name="pair_sum",
    )(*a, *b)


def outer_kernel(first_ref, mask_ref, *refs):
    parts, out_ref, tmp_ref = refs[:-2], refs[-2], refs[-1]
    mask = mask_ref[pl.ds(first_ref[0], 1), :].astype(jnp.float32)
    total = functools.reduce(lambda a, b: a + b, [r[...] for r in parts])
    rank = total.shape[1] // 2
    masked = total.T[rank:, :] * mask
    tmp_ref[...] = lax.dot_general(
        masked, total, (((1,), (0,)), ((), ())), preferred_element_type=jnp.float32, precision=HIGHEST
    )
    even = tmp_ref[pl.ds(0, rank // 2, stride=2), :]
    odd = tmp_ref[pl.ds(1, rank // 2, stride=2), :]
    out_ref[...] = jnp.concatenate([even[:, :rank], odd[:, :rank]], axis=1)


def outer(first, mask, parts):
    vmem = pl.BlockSpec(memory_space=pltpu.VMEM)
    rank = parts[0].shape[1] // 2
    return pl.pallas_call(
        outer_kernel,
        out_shape=jax.ShapeDtypeStruct((rank // 2, 2 * rank), jnp.float32),
        in_specs=[pl.BlockSpec(memory_space=pltpu.SMEM)] + [vmem] * (1 + len(parts)),
        out_specs=vmem,
        scratch_shapes=[pltpu.VMEM((rank, 2 * rank), jnp.float32)],
        compiler_params=pltpu.CompilerParams(vmem_limit_bytes=SMALL_VMEM),
        cost_estimate=pl.CostEstimate(flops=OUTER_FLOPS, bytes_accessed=0, transcendentals=0),
        name="outer",
    )(first, mask, *parts)


def sum_kernel(*refs):
    refs[-1][...] = functools.reduce(lambda a, b: a + b, [r[...] for r in refs[:-1]])


def sum_parts(parts):
    vmem = pl.BlockSpec(memory_space=pltpu.VMEM)
    return pl.pallas_call(
        sum_kernel,
        out_shape=jax.ShapeDtypeStruct(parts[0].shape, jnp.float32),
        in_specs=[vmem] * len(parts),
        out_specs=vmem,
        compiler_params=pltpu.CompilerParams(vmem_limit_bytes=SMALL_VMEM),
        cost_estimate=NO_COST,
        name="sum_parts",
    )(*parts)


def add_blocks(dots, squares, unit_ref, q_ref, y, rows):
    for z in range(q_ref.shape[0]):
        q = q_ref[z].astype(jnp.float32)
        dots += q * unit_ref[pl.ds(z * rows + y, 1), :]
        squares += q * q
    return dots, squares


def start_kernel(rows, ks, y_ref, a_ref, b_ref, *refs):
    q_refs, (unit_ref, dots_ref, squares_ref) = refs[:-3], refs[-3:]
    grad = a_ref[...] + b_ref[...]
    mean = jnp.sum(grad * grad, keepdims=True) / grad.size
    unit_ref[...] = (grad / jnp.sqrt(mean + 1e-06)).astype(jnp.bfloat16).astype(jnp.float32)
    dots = squares = jnp.zeros(dots_ref.shape, jnp.float32)
    for k, q_ref in zip(ks, q_refs):
        dots, squares = add_blocks(dots, squares, unit_ref, q_ref, jnp.bitwise_xor(y_ref[0], k), rows)
    dots_ref[...] = dots
    squares_ref[...] = squares


def score_start(y, parts, q, ks, rows):
    vmem = pl.BlockSpec(memory_space=pltpu.VMEM)
    sums = jax.ShapeDtypeStruct(q[0].shape[1:], jnp.float32)
    return pl.pallas_call(
        functools.partial(start_kernel, rows, ks),
        out_shape=[jax.ShapeDtypeStruct(parts[0].shape, jnp.float32), sums, sums],
        in_specs=[pl.BlockSpec(memory_space=pltpu.SMEM)] + [vmem] * (len(parts) + len(q)),
        out_specs=[vmem] * 3,
        compiler_params=pltpu.CompilerParams(vmem_limit_bytes=SMALL_VMEM),
        cost_estimate=NO_COST,
        name="score_start",
    )(y, *parts, *q)


def score_kernel(rank, rows, k, ids_ref, unit_ref, dots_ref, squares_ref, q_ref, out_ref):
    y = jnp.bitwise_xor(ids_ref[2], k)
    dots, squares = add_blocks(dots_ref[...], squares_ref[...], unit_ref, q_ref, y, rows)
    dots, squares = [jnp.sum(x.T, axis=0, keepdims=True) for x in (dots, squares)]
    scores = dots / (rank * jnp.sqrt(squares / unit_ref.size + 1e-06))
    index = ids_ref[1] + lax.broadcasted_iota(jnp.int32, scores.shape, 1)
    out_ref[...] = jnp.where(index == ids_ref[0], 0.0, scores)


def score(rank, rows, ids, started, q, k):
    vmem = pl.BlockSpec(memory_space=pltpu.VMEM)
    return pl.pallas_call(
        functools.partial(score_kernel, rank, rows, k),
        out_shape=jax.ShapeDtypeStruct((1, q.shape[1]), jnp.float32),
        in_specs=[pl.BlockSpec(memory_space=pltpu.SMEM)] + [vmem] * 4,
        out_specs=vmem,
        compiler_params=pltpu.CompilerParams(vmem_limit_bytes=SMALL_VMEM),
        cost_estimate=NO_COST,
        name="score",
    )(ids, *started, q)


def hops(k):
    return 2 if k == 2 else 1


def body(hidden_in, out_grad, proj_in, proj_out, token_mask, cand_ids, queries):
    rank = proj_in.shape[1]
    devices = lax.axis_size("tensor")
    chips = devices // 2
    dp = lax.axis_size("dp")
    me = lax.axis_index("tensor").astype(jnp.int32)
    core, chip = me % 2, me // 2
    qlocal, qcols = queries.shape

    def swap(x, mask):
        return lax.ppermute(x, "tensor", [(i, i ^ mask) for i in range(devices)])

    with jax.named_scope("gather_queries"):
        layers = dp // ROWS
        columns = [[z * ROWS + y for z in range(layers)] for y in range(ROWS)]
        copies = jnp.broadcast_to(queries[None], (layers, *queries.shape))
        column = lax.all_to_all(copies, "dp", 0, 0, tiled=True, axis_index_groups=columns)
        near = 1
        others = [k for k in range(1, ROWS) if k != near]
        gathered = [column] + [
            lax.ppermute(column, "dp", [(i, i ^ k) for i in range(dp)]) for k in (*others, near)
        ]

    with jax.named_scope("project"):
        theirs, kept = project_theirs(jnp.stack([core, chip]), hidden_in, out_grad, proj_in.T, proj_out.T)
        arrived = [swap(part, 1) for part in theirs]
        mine = project_mine(*kept)
    with jax.named_scope("exchange_tokens"):
        blocks = pair_sum(mine, arrived)
        order = sorted(range(1, chips), key=hops, reverse=True)
        parts = [blocks[0]] + [swap(blocks[k], 2 * k) for k in order]
    with jax.named_scope("outer"):
        first = (core * chips + chip)[None]
        partial = outer(first, token_mask.reshape(-1, BLOCK), parts)
    with jax.named_scope("exchange_grad"):
        pair = sum_parts([partial, swap(partial, 1)])
        four = sum_parts([pair, swap(pair, 2)])
        partials = [four, swap(four, 6)]
    with jax.named_scope("score"):
        row = lax.axis_index("dp").astype(jnp.int32) % ROWS
        started = score_start(row[None], partials, gathered[:-1], (0, *others), ROWS)
        ids = jnp.stack([cand_ids[0], me * qlocal, row])
        return score(rank, ROWS, ids, started, gathered[-1], near)


def solution(mesh):
    placed = (
        P("dp", "tensor"),
        P("dp", "tensor"),
        P("tensor", None),
        P("tensor", None),
        P("dp"),
        P("dp"),
        P("tensor", "dp"),
    )
    return jax.shard_map(
        body, mesh=mesh, in_specs=placed, out_specs=P("dp", "tensor"), check_vma=False
    )
```

profile of v0, /device:TPU:56, one launch (start us, length us, event | category | flops | bytes accessed | tf_op | source)
XLA Modules:
  0.0 39.9 jit_solution(4372617774031888942)
XLA Ops:
  0.0 1.5 %broadcast_in_dim.5 = bf16[8,128,128]{2,1,0:T(8,128)(2,1)} broadcast(bf16[128,128]{1,0:T(8,128)(2,1)} %param.13), dimensions={1,2} | broadcast | bytes 294912 | tf_op jit(solution)/shard_map/gather_queries/broadcast_in_dim | solution.py:256
  1.5 8.6 %all-to-all-start = ((bf16[8,128,128]{2,1,0:T(8,128)(2,1)}), bf16[8,128,128]{2,1,0:T(8,128)(2,1)S(1)}, u32[]{:S(2)}, u32[]{:S(2)}) async-start(bf16[8,128,128]{2,1,0:T(8,128)(2,1)} %broadcast_in_dim.5), calls=%async_computation | async-start | bytes 524288 | tf_op jit(solution)/shard_map/gather_queries/all_to_all | solution.py:257
  10.1 0.1 pad_add_fusion.1.place_ref
  10.1 5.0 %project_theirs.1 = (f32[256,128]{1,0:T(8,128)S(1)}, f32[256,128]{1,0:T(8,128)S(1)}, f32[256,128]{1,0:T(8,128)S(1)}, f32[256,128]{1,0:T(8,128)S(1)}, bf16[1024,1...) custom-call(s32[2]{0:T(128)S(1)} %pad_add_fusion.1.place_ref, ...), custom_call_target="tpu_custom_call" | custom-call | tf_op jit(solution)/shard_map/project/project_theirs/pallas_call | solution.py:72
  15.2 0.0 copy-start
  15.2 0.1 collective-permute-start
  15.3 0.5 %collective-permute-start.1 = (f32[256,128]{1,0:T(8,128)S(1)}, f32[256,128]{1,0:T(8,128)S(1)}, u32[]{:S(2)}, u32[]{:S(2)}) collective-permute-start(f32[256,128]{1,0:T(8,128)S(1)} %get-tuple-element.31), channel_id=1, source_target_pairs={{0,1},{1,0},{2,3},{3,2},{4,5},{5,4},{6,7},{7,6},{8,9},{9,8},{10,11... | collective-permute-start | bytes 393224 | tf_op jit(solution)/shard_map/project/ppermute | solution.py:251
  15.8 0.1 collective-permute-start.2
  15.9 0.4 %collective-permute-start.3 = (f32[256,128]{1,0:T(8,128)S(1)}, f32[256,128]{1,0:T(8,128)S(1)}, u32[]{:S(2)}, u32[]{:S(2)}) collective-permute-start(f32[256,128]{1,0:T(8,128)S(1)} %get-tuple-element.33), channel_id=1, source_target_pairs={{0,1},{1,0},{2,3},{3,2},{4,5},{5,4},{6,7},{7,6},{8,9},{9,8},{10,11... | collective-permute-start | bytes 393224 | tf_op jit(solution)/shard_map/project/ppermute | solution.py:251
  16.3 1.4 %project_mine.1 = (f32[256,128]{1,0:T(8,128)S(1)}, f32[256,128]{1,0:T(8,128)S(1)}, f32[256,128]{1,0:T(8,128)S(1)}, f32[256,128]{1,0:T(8,128)S(1)}) custom-call(bf16[1024,1792]{1,0:T(8,128)(2,1)S(1)} %get-tuple-element.23.hidden_ref, bf16[1024,512]{1,0:T(8,128)(2,1)S(1)} %get-tuple-element.24.grad_ref, bf16[128,2304]{1,0:T(8,128)(2,1)S(1)} %get-tuple-element.25.w_ref), custom_call_target="tpu_custom_call" | custom-call | tf_op jit(solution)/shard_map/project/project_mine/pallas_call | solution.py:105
  17.7 0.0 collective-permute-done.refs_4_
  17.7 0.0 collective-permute-done.2.refs_6_
  17.7 0.1 pair_sum.1
  17.8 3.1 %collective-permute-start.4 = (f32[256,128]{1,0:T(8,128)S(1)}, f32[256,128]{1,0:T(8,128)S(1)}, u32[]{:S(2)}, u32[]{:S(2)}) collective-permute-start(f32[256,128]{1,0:T(8,128)S(1)} %get-tuple-element.35), channel_id=1, source_target_pairs={{0,4},{1,5},{2,6},{3,7},{4,0},{5,1},{6,2},{7,3},{8,12},{9,13},{10,... | collective-permute-start | bytes 393224 | tf_op jit(solution)/shard_map/exchange_tokens/ppermute | solution.py:251
  20.9 0.6 %collective-permute-start.5 = (f32[256,128]{1,0:T(8,128)S(1)}, f32[256,128]{1,0:T(8,128)S(1)}, u32[]{:S(2)}, u32[]{:S(2)}) collective-permute-start(f32[256,128]{1,0:T(8,128)S(1)} %get-tuple-element.36), channel_id=1, source_target_pairs={{0,2},{1,3},{2,0},{3,1},{4,6},{5,7},{6,4},{7,5},{8,10},{9,11},{10,... | collective-permute-start | bytes 393224 | tf_op jit(solution)/shard_map/exchange_tokens/ppermute | solution.py:251
  21.5 0.5 %collective-permute-start.6 = (f32[256,128]{1,0:T(8,128)S(1)}, f32[256,128]{1,0:T(8,128)S(1)}, u32[]{:S(2)}, u32[]{:S(2)}) collective-permute-start(f32[256,128]{1,0:T(8,128)S(1)} %get-tuple-element.37), channel_id=1, source_target_pairs={{0,6},{1,7},{2,4},{3,5},{4,2},{5,3},{6,0},{7,1},{8,14},{9,15},{10,... | collective-permute-start | bytes 393224 | tf_op jit(solution)/shard_map/exchange_tokens/ppermute | solution.py:251
  22.1 1.3 %collective-permute-start.10 = (bf16[8,128,128]{2,1,0:T(8,128)(2,1)S(1)}, bf16[8,128,128]{2,1,0:T(8,128)(2,1)S(1)}, u32[]{:S(2)}, u32[]{:S(2)}) collective-permute-start(bf16[8,128,128]{2,1,0:T(8,128)(2,1)S(1)} %all-to-all-done.refs_0_), channel_id=1, source_target_pairs={{0,16},{8,24},{16,0},{24,8},{32,48},{40,56},{48,32},{56,40},{64,80... | collective-permute-start | bytes 786440 | tf_op jit(solution)/shard_map/gather_queries/ppermute | solution.py:261
  23.4 2.2 %collective-permute-start.11 = (bf16[8,128,128]{2,1,0:T(8,128)(2,1)S(1)}, bf16[8,128,128]{2,1,0:T(8,128)(2,1)S(1)}, u32[]{:S(2)}, u32[]{:S(2)}) collective-permute-start(bf16[8,128,128]{2,1,0:T(8,128)(2,1)S(1)} %all-to-all-done.refs_0_), channel_id=1, source_target_pairs={{0,24},{8,16},{16,8},{24,0},{32,56},{40,48},{48,40},{56,32},{64,88... | collective-permute-start | bytes 786440 | tf_op jit(solution)/shard_map/gather_queries/ppermute | solution.py:261
  25.6 0.2 collective-permute-done.4.refs_1_
  25.7 0.7 %collective-permute-start.12 = (bf16[8,128,128]{2,1,0:T(8,128)(2,1)S(1)}, bf16[8,128,128]{2,1,0:T(8,128)(2,1)S(1)}, u32[]{:S(2)}, u32[]{:S(2)}) collective-permute-start(bf16[8,128,128]{2,1,0:T(8,128)(2,1)S(1)} %all-to-all-done.refs_0_), channel_id=1, source_target_pairs={{0,8},{8,0},{16,24},{24,16},{32,40},{40,32},{48,56},{56,48},{64,72... | collective-permute-start | bytes 786440 | tf_op jit(solution)/shard_map/gather_queries/ppermute | solution.py:261
  26.5 1.3 %collective-permute-done.5.refs_2_ = f32[256,128]{1,0:T(8,128)S(1)} collective-permute-done((f32[256,128]{1,0:T(8,128)S(1)}, f32[256,128]{1,0:T(8,128)S(1)}, u32[]{:S(2)}, u32[]{:S(2)}) %collective-permute-start.5) | collective-permute-done | bytes 131104 | tf_op jit(solution)/shard_map/exchange_tokens/ppermute | solution.py:251
  27.8 0.3 collective-permute-done.6.refs_3_
  28.1 0.4 outer.1.refs_0_
  28.4 0.0 collective-permute-start.7
  28.5 1.2 %collective-permute-done.7.refs_1_ = f32[32,128]{1,0:T(8,128)S(1)} collective-permute-done((f32[32,128]{1,0:T(8,128)S(1)}, f32[32,128]{1,0:T(8,128)S(1)}, u32[]{:S(2)}, u32[]{:S(2)}) %collective-permute-start.7) | collective-permute-done | bytes 16416 | tf_op jit(solution)/shard_map/exchange_grad/ppermute | solution.py:251
  29.7 1.1 %collective-permute-start.8 = (f32[32,128]{1,0:T(8,128)S(1)}, f32[32,128]{1,0:T(8,128)S(1)}, u32[]{:S(2)}, u32[]{:S(2)}) collective-permute-start(f32[32,128]{1,0:T(8,128)S(1)} %sum_parts.2.refs_0_), channel_id=1, source_target_pairs={{0,2},{1,3},{2,0},{3,1},{4,6},{5,7},{6,4},{7,5},{8,10},{9,11},{10,... | collective-permute-start | bytes 49160 | tf_op jit(solution)/shard_map/exchange_grad/ppermute | solution.py:251
  31.4 2.0 %collective-permute-done.8.refs_1_ = f32[32,128]{1,0:T(8,128)S(1)} collective-permute-done((f32[32,128]{1,0:T(8,128)S(1)}, f32[32,128]{1,0:T(8,128)S(1)}, u32[]{:S(2)}, u32[]{:S(2)}) %collective-permute-start.8) | collective-permute-done | bytes 16416 | tf_op jit(solution)/shard_map/exchange_grad/ppermute | solution.py:251
  33.4 2.4 %collective-permute-start.9 = (f32[32,128]{1,0:T(8,128)S(1)}, f32[32,128]{1,0:T(8,128)S(1)}, u32[]{:S(2)}, u32[]{:S(2)}) collective-permute-start(f32[32,128]{1,0:T(8,128)S(1)} %sum_parts.3.a_ref), channel_id=1, source_target_pairs={{0,6},{1,7},{2,4},{3,5},{4,2},{5,3},{6,0},{7,1},{8,14},{9,15},{10,... | collective-permute-start | bytes 49160 | tf_op jit(solution)/shard_map/exchange_grad/ppermute | solution.py:251
  35.8 0.1 pad_add_fusion.ids_ref
  35.8 2.5 %collective-permute-done.9.b_ref = f32[32,128]{1,0:T(8,128)S(1)} collective-permute-done((f32[32,128]{1,0:T(8,128)S(1)}, f32[32,128]{1,0:T(8,128)S(1)}, u32[]{:S(2)}, u32[]{:S(2)}) %collective-permute-start.9) | collective-permute-done | bytes 16416 | tf_op jit(solution)/shard_map/exchange_grad/ppermute | solution.py:251
  38.4 0.3 score_start.1
  38.7 1.2 %score.1 = f32[1,128]{1,0:T(1,128)} custom-call(s32[3]{0:T(128)S(1)} %pad_add_fusion.ids_ref, f32[32,128]{1,0:T(8,128)S(1)} %get-tuple-element.38.unit_ref, f32[128,128]{1,0:T(8,128)S(1)} %get-tuple-element.39.dots_ref, f32[128,128]{1,0:T(8,128)S(1)} %get-tuple-element.40.squares_ref, bf16[8,128,128]{2,1,0:T(8,128)(2,1)S(1)} %collective-permute-done.12.q_ref), custom_call_target="tpu_custom_call" | custom-call | tf_op jit(solution)/shard_map/score/score/pallas_call | solution.py:226
  (10 shorter events, 0.0 us)
Async XLA Ops:
  1.5 20.6 %all-to-all-start = ((bf16[8,128,128]{2,1,0:T(8,128)(2,1)}), bf16[8,128,128]{2,1,0:T(8,128)(2,1)S(1)}, u32[]{:S(2)}, u32[]{:S(2)}) async-start(bf16[8,128,128]{2,1,0:T(8,128)(2,1)} %broadcast_in_dim.5), calls=%async_computation | async-start | bytes 524288 | tf_op jit(solution)/shard_map/gather_queries/all_to_all | solution.py:257
  15.2 6.9 %copy-start = (s32[2048]{0:T(1024)S(1)}, s32[2048]{0:T(1024)}, u32[]{:S(2)}) copy-start(s32[2048]{0:T(1024)} %param.11) | copy-start | bytes 24580
  15.2 2.5 %collective-permute-start = (f32[256,128]{1,0:T(8,128)S(1)}, f32[256,128]{1,0:T(8,128)S(1)}, u32[]{:S(2)}, u32[]{:S(2)}) collective-permute-start(f32[256,128]{1,0:T(8,128)S(1)} %get-tuple-element.30), channel_id=1, source_target_pairs={{0,1},{1,0},{2,3},{3,2},{4,5},{5,4},{6,7},{7,6},{8,9},{9,8},{10,11... | collective-permute-start | bytes 393224 | tf_op jit(solution)/shard_map/project/ppermute | solution.py:251
  15.3 2.4 %collective-permute-start.1 = (f32[256,128]{1,0:T(8,128)S(1)}, f32[256,128]{1,0:T(8,128)S(1)}, u32[]{:S(2)}, u32[]{:S(2)}) collective-permute-start(f32[256,128]{1,0:T(8,128)S(1)} %get-tuple-element.31), channel_id=1, source_target_pairs={{0,1},{1,0},{2,3},{3,2},{4,5},{5,4},{6,7},{7,6},{8,9},{9,8},{10,11... | collective-permute-start | bytes 393224 | tf_op jit(solution)/shard_map/project/ppermute | solution.py:251
  15.8 1.9 %collective-permute-start.2 = (f32[256,128]{1,0:T(8,128)S(1)}, f32[256,128]{1,0:T(8,128)S(1)}, u32[]{:S(2)}, u32[]{:S(2)}) collective-permute-start(f32[256,128]{1,0:T(8,128)S(1)} %get-tuple-element.32), channel_id=1, source_target_pairs={{0,1},{1,0},{2,3},{3,2},{4,5},{5,4},{6,7},{7,6},{8,9},{9,8},{10,11... | collective-permute-start | bytes 393224 | tf_op jit(solution)/shard_map/project/ppermute | solution.py:251
  15.9 1.8 %collective-permute-start.3 = (f32[256,128]{1,0:T(8,128)S(1)}, f32[256,128]{1,0:T(8,128)S(1)}, u32[]{:S(2)}, u32[]{:S(2)}) collective-permute-start(f32[256,128]{1,0:T(8,128)S(1)} %get-tuple-element.33), channel_id=1, source_target_pairs={{0,1},{1,0},{2,3},{3,2},{4,5},{5,4},{6,7},{7,6},{8,9},{9,8},{10,11... | collective-permute-start | bytes 393224 | tf_op jit(solution)/shard_map/project/ppermute | solution.py:251
  17.8 7.9 %collective-permute-start.4 = (f32[256,128]{1,0:T(8,128)S(1)}, f32[256,128]{1,0:T(8,128)S(1)}, u32[]{:S(2)}, u32[]{:S(2)}) collective-permute-start(f32[256,128]{1,0:T(8,128)S(1)} %get-tuple-element.35), channel_id=1, source_target_pairs={{0,4},{1,5},{2,6},{3,7},{4,0},{5,1},{6,2},{7,3},{8,12},{9,13},{10,... | collective-permute-start | bytes 393224 | tf_op jit(solution)/shard_map/exchange_tokens/ppermute | solution.py:251
  20.9 6.9 %collective-permute-start.5 = (f32[256,128]{1,0:T(8,128)S(1)}, f32[256,128]{1,0:T(8,128)S(1)}, u32[]{:S(2)}, u32[]{:S(2)}) collective-permute-start(f32[256,128]{1,0:T(8,128)S(1)} %get-tuple-element.36), channel_id=1, source_target_pairs={{0,2},{1,3},{2,0},{3,1},{4,6},{5,7},{6,4},{7,5},{8,10},{9,11},{10,... | collective-permute-start | bytes 393224 | tf_op jit(solution)/shard_map/exchange_tokens/ppermute | solution.py:251
  21.5 6.6 %collective-permute-start.6 = (f32[256,128]{1,0:T(8,128)S(1)}, f32[256,128]{1,0:T(8,128)S(1)}, u32[]{:S(2)}, u32[]{:S(2)}) collective-permute-start(f32[256,128]{1,0:T(8,128)S(1)} %get-tuple-element.37), channel_id=1, source_target_pairs={{0,6},{1,7},{2,4},{3,5},{4,2},{5,3},{6,0},{7,1},{8,14},{9,15},{10,... | collective-permute-start | bytes 393224 | tf_op jit(solution)/shard_map/exchange_tokens/ppermute | solution.py:251
  22.1 16.3 %collective-permute-start.10 = (bf16[8,128,128]{2,1,0:T(8,128)(2,1)S(1)}, bf16[8,128,128]{2,1,0:T(8,128)(2,1)S(1)}, u32[]{:S(2)}, u32[]{:S(2)}) collective-permute-start(bf16[8,128,128]{2,1,0:T(8,128)(2,1)S(1)} %all-to-all-done.refs_0_), channel_id=1, source_target_pairs={{0,16},{8,24},{16,0},{24,8},{32,48},{40,56},{48,32},{56,40},{64,80... | collective-permute-start | bytes 786440 | tf_op jit(solution)/shard_map/gather_queries/ppermute | solution.py:261
  23.4 15.0 %collective-permute-start.11 = (bf16[8,128,128]{2,1,0:T(8,128)(2,1)S(1)}, bf16[8,128,128]{2,1,0:T(8,128)(2,1)S(1)}, u32[]{:S(2)}, u32[]{:S(2)}) collective-permute-start(bf16[8,128,128]{2,1,0:T(8,128)(2,1)S(1)} %all-to-all-done.refs_0_), channel_id=1, source_target_pairs={{0,24},{8,16},{16,8},{24,0},{32,56},{40,48},{48,40},{56,32},{64,88... | collective-permute-start | bytes 786440 | tf_op jit(solution)/shard_map/gather_queries/ppermute | solution.py:261
  25.7 13.0 %collective-permute-start.12 = (bf16[8,128,128]{2,1,0:T(8,128)(2,1)S(1)}, bf16[8,128,128]{2,1,0:T(8,128)(2,1)S(1)}, u32[]{:S(2)}, u32[]{:S(2)}) collective-permute-start(bf16[8,128,128]{2,1,0:T(8,128)(2,1)S(1)} %all-to-all-done.refs_0_), channel_id=1, source_target_pairs={{0,8},{8,0},{16,24},{24,16},{32,40},{40,32},{48,56},{56,48},{64,72... | collective-permute-start | bytes 786440 | tf_op jit(solution)/shard_map/gather_queries/ppermute | solution.py:261
  28.4 1.2 %collective-permute-start.7 = (f32[32,128]{1,0:T(8,128)S(1)}, f32[32,128]{1,0:T(8,128)S(1)}, u32[]{:S(2)}, u32[]{:S(2)}) collective-permute-start(f32[32,128]{1,0:T(8,128)S(1)} %outer.1.refs_0_), channel_id=1, source_target_pairs={{0,1},{1,0},{2,3},{3,2},{4,5},{5,4},{6,7},{7,6},{8,9},{9,8},{10,11... | collective-permute-start | bytes 49160 | tf_op jit(solution)/shard_map/exchange_grad/ppermute | solution.py:251
  29.7 3.7 %collective-permute-start.8 = (f32[32,128]{1,0:T(8,128)S(1)}, f32[32,128]{1,0:T(8,128)S(1)}, u32[]{:S(2)}, u32[]{:S(2)}) collective-permute-start(f32[32,128]{1,0:T(8,128)S(1)} %sum_parts.2.refs_0_), channel_id=1, source_target_pairs={{0,2},{1,3},{2,0},{3,1},{4,6},{5,7},{6,4},{7,5},{8,10},{9,11},{10,... | collective-permute-start | bytes 49160 | tf_op jit(solution)/shard_map/exchange_grad/ppermute | solution.py:251
  33.4 4.9 %collective-permute-start.9 = (f32[32,128]{1,0:T(8,128)S(1)}, f32[32,128]{1,0:T(8,128)S(1)}, u32[]{:S(2)}, u32[]{:S(2)}) collective-permute-start(f32[32,128]{1,0:T(8,128)S(1)} %sum_parts.3.a_ref), channel_id=1, source_target_pairs={{0,6},{1,7},{2,4},{3,5},{4,2},{5,3},{6,0},{7,1},{8,14},{9,15},{10,... | collective-permute-start | bytes 49160 | tf_op jit(solution)/shard_map/exchange_grad/ppermute | solution.py:251
where the time goes:
time: 40.2 us; the launch traced here: 39.9 us
  starting transfers between devices  21.7 us (54%)
  Pallas kernels  8.4 us (21%)
  waiting for transfers between devices  7.45 us (19%)
  local copies, waits for them, and re-layouts  1.49 us (4%)
  between operations  0.77 us (2%)
    ppermute x10, starting transfers between devices, swap(): return lax.ppermute(x, 'tensor', [(i, i ^ mask) for i in range(devices)])  8.87 us
    all_to_all x1, starting transfers between devices, body(): lax.all_to_all(copies, 'dp', 0, 0, tiled=True, axis_index_groups=columns)  8.57 us
    ppermute x10, waiting for transfers between devices, swap(): return lax.ppermute(x, 'tensor', [(i, i ^ mask) for i in range(devices)])  7.44 us
    pallas_call x1, Pallas kernels, project_theirs(): pl.pallas_call(functools.partial(theirs_kernel, n), out_shape=[jax.ShapeD...  5.05 us
    ppermute x3, starting transfers between devices, body(): lax.ppermute(column, 'dp', [(i, i ^ k) for i in range(dp)])  4.25 us
    broadcast_in_dim x1, local copies, waits for them, and re-layouts, body(): copies = jnp.broadcast_to(queries[None], (layers, *queries.shape))  1.48 us
    pallas_call x1, Pallas kernels, project_mine(): pl.pallas_call(mine_kernel, out_shape=[jax.ShapeDtypeStruct((BLOCK, w.sha...  1.36 us
    pallas_call x1, Pallas kernels, score(): pl.pallas_call(functools.partial(score_kernel, rank, rows, k), out_shape=...  1.23 us
  transfers between devices with their start and end apart: 14, of which 6 were waited for; matrix products, arithmetic and copies ran while one was open for 0% of the time, Pallas kernels for 18%

commit v1 on v0

v1 whole, which is shorter than its diff:
```python
import functools

import jax
import jax.numpy as jnp
from jax import lax
from jax.experimental import pallas as pl
from jax.experimental.pallas import tpu as pltpu
from jax.sharding import PartitionSpec as P

BLOCK = 256
EACH = 2
OUTER_FLOPS = 4 << 30
PROJECT_VMEM = 16 << 20
SMALL_VMEM = 8 << 20
ROWS = 4
ROW_ORDER = (0, 2, 3, 1)
NO_COST = pl.CostEstimate(flops=0, bytes_accessed=0, transcendentals=0)
HIGHEST = lax.Precision.HIGHEST


def nt_dot(a, b, precision=None):
    return lax.dot_general(
        a, b, (((1,), (1,)), ((), ())), preferred_element_type=jnp.float32, precision=precision
    )


def project_block(hidden, grad, w):
    width = hidden.shape[1]
    return nt_dot(hidden, w[:, :width]) + nt_dot(grad, w[:, width:])


def theirs_kernel(n, core_ref, chip_ref, hidden_ref, grad_ref, pin_ref, pout_ref, *refs):
    outs, (own_hidden, own_grad, w_ref, hidden, grad, sem, w_sem) = refs[:-7], refs[-7:]
    rank, width = pin_ref.shape
    depth = pout_ref.shape[1]
    weights = [
        pltpu.make_async_copy(pin_ref, w_ref.at[pl.ds(0, rank), pl.ds(0, width)], w_sem.at[0]),
        pltpu.make_async_copy(pout_ref, w_ref.at[pl.ds(rank, rank), pl.ds(width, depth)], w_sem.at[1]),
    ]
    copies = []
    for j, (half, buffers) in enumerate(((1 - core_ref[0], (hidden, grad)), (core_ref[0], (own_hidden, own_grad)))):
        for k in range(n):
            first = (half * n + jnp.bitwise_xor(chip_ref[0], k)) * BLOCK
            rows = pl.ds(pl.multiple_of(first, BLOCK), BLOCK)
            for i, (source, buffer) in enumerate(zip((hidden_ref, grad_ref), buffers)):
                copies.append(
                    pltpu.make_async_copy(source.at[rows, :], buffer.at[pl.ds(k * BLOCK, BLOCK), :], sem.at[j, k, i])
                )
    for copy in weights + copies[: 2 * n]:
        copy.start()
    w_ref[rank:, :width] = jnp.zeros((rank, width), w_ref.dtype)
    w_ref[:rank, width:] = jnp.zeros((rank, depth), w_ref.dtype)
    for copy in weights:
        copy.wait()
    for copy in copies[2 * n :]:
        copy.start()
    for copy in copies[: 2 * n]:
        copy.wait()
    for k in range(n):
        rows = pl.ds(k * BLOCK, BLOCK)
        outs[k // EACH][pl.ds(k % EACH * BLOCK, BLOCK), :] = project_block(hidden[rows, :], grad[rows, :], w_ref)
    for copy in copies[2 * n :]:
        copy.wait()


def project_theirs(core, chip, hidden, grad, pin_t, pout_t):
    rank, width = pin_t.shape
    depth = pout_t.shape[1]
    half = hidden.shape[0] // 2
    n = half // BLOCK
    messages = n // EACH
    vmem = pl.BlockSpec(memory_space=pltpu.VMEM)
    hbm = pl.BlockSpec(memory_space=pltpu.HBM)
    held = [pltpu.with_memory_space_constraint(x, pltpu.HBM) for x in (hidden, grad, pin_t, pout_t)]
    outs = pl.pallas_call(
        functools.partial(theirs_kernel, n),
        out_shape=[jax.ShapeDtypeStruct((EACH * BLOCK, 2 * rank), jnp.float32)] * messages
        + [
            pltpu.VMEM((half, width), hidden.dtype),
            pltpu.VMEM((half, depth), grad.dtype),
            pltpu.VMEM((2 * rank, width + depth), pin_t.dtype),
        ],
        in_specs=[pl.BlockSpec(memory_space=pltpu.SMEM)] * 2 + [hbm] * 4,
        out_specs=[vmem] * (messages + 3),
        scratch_shapes=[
            pltpu.VMEM((half, width), hidden.dtype),
            pltpu.VMEM((half, depth), grad.dtype),
            pltpu.SemaphoreType.DMA((2, n, 2)),
            pltpu.SemaphoreType.DMA((2,)),
        ],
        compiler_params=pltpu.CompilerParams(vmem_limit_bytes=PROJECT_VMEM),
        cost_estimate=NO_COST,
        name="project_theirs",
    )(core[None], chip[None], *held)
    return outs[:messages], outs[messages:]


def mine_kernel(hidden_ref, grad_ref, w_ref, *outs):
    for k, out in enumerate(outs):
        rows = pl.ds(k * BLOCK, BLOCK)
        out[...] = project_block(hidden_ref[rows, :], grad_ref[rows, :], w_ref)


def project_mine(hidden, grad, w):
    n = hidden.shape[0] // BLOCK
    vmem = pl.BlockSpec(memory_space=pltpu.VMEM)
    held = [pltpu.with_memory_space_constraint(x, pltpu.VMEM) for x in (hidden, grad, w)]
    return pl.pallas_call(
        mine_kernel,
        out_shape=[jax.ShapeDtypeStruct((BLOCK, w.shape[0]), jnp.float32)] * n,
        in_specs=[vmem] * 3,
        out_specs=[vmem] * n,
        compiler_params=pltpu.CompilerParams(vmem_limit_bytes=SMALL_VMEM),
        cost_estimate=NO_COST,
        name="project_mine",
    )(*held)


def pair_kernel(n, *refs):
    mine, arrived, outs = refs[:n], refs[n:-n], refs[-n:]
    for k, out in enumerate(outs):
        out[...] = mine[k][...] + arrived[k // EACH][pl.ds(k % EACH * BLOCK, BLOCK), :]


def pair_sum(mine, arrived):
    vmem = pl.BlockSpec(memory_space=pltpu.VMEM)
    return pl.pallas_call(
        functools.partial(pair_kernel, len(mine)),
        out_shape=[jax.ShapeDtypeStruct(x.shape, x.dtype) for x in mine],
        in_specs=[vmem] * (len(mine) + len(arrived)),
        out_specs=[vmem] * len(mine),
        compiler_params=pltpu.CompilerParams(vmem_limit_bytes=SMALL_VMEM),
        cost_estimate=NO_COST,
        name="pair_sum",
    )(*mine, *arrived)


def outer_kernel(block_ref, row_ref, mask_ref, *refs):
    parts, (out_ref, tmp_ref, both_ref) = refs[:-3], refs[-3:]
    mask = mask_ref[pl.ds(block_ref[0], 1), :].astype(jnp.float32)
    total = functools.reduce(lambda a, b: a + b, [r[...] for r in parts])
    rank = total.shape[1] // 2
    masked = total.T[rank:, :] * mask
    tmp_ref[...] = lax.dot_general(
        masked, total, (((1,), (0,)), ((), ())), preferred_element_type=jnp.float32, precision=HIGHEST
    )
    even = tmp_ref[pl.ds(0, rank // 2, stride=2), :]
    odd = tmp_ref[pl.ds(1, rank // 2, stride=2), :]
    both_ref[...] = jnp.concatenate([even[:, :rank], odd[:, :rank]], axis=1)
    layers = out_ref.shape[0] // ROWS
    for k, other in enumerate(ROW_ORDER):
        row = jnp.bitwise_xor(row_ref[0], other)
        out_ref[pl.ds(k * layers, layers), :] = both_ref[pl.ds(row, layers, stride=ROWS), :]


def outer(block, y, mask, parts):
    vmem = pl.BlockSpec(memory_space=pltpu.VMEM)
    rank = parts[0].shape[1] // 2
    return pl.pallas_call(
        outer_kernel,
        out_shape=jax.ShapeDtypeStruct((rank // 2, 2 * rank), jnp.float32),
        in_specs=[pl.BlockSpec(memory_space=pltpu.SMEM)] * 2 + [vmem] * (1 + len(parts)),
        out_specs=vmem,
        scratch_shapes=[pltpu.VMEM((rank, 2 * rank), jnp.float32), pltpu.VMEM((rank // 2, 2 * rank), jnp.float32)],
        compiler_params=pltpu.CompilerParams(vmem_limit_bytes=SMALL_VMEM),
        cost_estimate=pl.CostEstimate(flops=OUTER_FLOPS, bytes_accessed=0, transcendentals=0),
        name="outer",
    )(block[None], y[None], mask, *parts)


def sum_kernel(*refs):
    refs[-1][...] = functools.reduce(lambda a, b: a + b, [r[...] for r in refs[:-1]])


def sum_parts(parts):
    vmem = pl.BlockSpec(memory_space=pltpu.VMEM)
    return pl.pallas_call(
        sum_kernel,
        out_shape=jax.ShapeDtypeStruct(parts[0].shape, jnp.float32),
        in_specs=[vmem] * len(parts),
        out_specs=vmem,
        compiler_params=pltpu.CompilerParams(vmem_limit_bytes=SMALL_VMEM),
        cost_estimate=NO_COST,
        name="sum_parts",
    )(*parts)


def add_blocks(dots, squares, unit, q_ref):
    for z in range(q_ref.shape[0]):
        q = q_ref[z].astype(jnp.float32)
        dots += q * unit[z : z + 1, :]
        squares += q * q
    return dots, squares


def start_kernel(a_ref, b_ref, *refs):
    q_refs, (last_ref, dots_ref, squares_ref) = refs[:-3], refs[-3:]
    grad = a_ref[...] + b_ref[...]
    mean = jnp.sum(grad * grad, keepdims=True) / grad.size
    unit = (grad / jnp.sqrt(mean + 1e-06)).astype(jnp.bfloat16).astype(jnp.float32)
    layers = q_refs[0].shape[0]
    dots = squares = jnp.zeros(dots_ref.shape, jnp.float32)
    for k, q_ref in enumerate(q_refs):
        dots, squares = add_blocks(dots, squares, unit[k * layers : (k + 1) * layers, :], q_ref)
    dots_ref[...] = dots
    squares_ref[...] = squares
    last_ref[...] = unit[len(q_refs) * layers :, :]


def score_start(parts, q):
    vmem = pl.BlockSpec(memory_space=pltpu.VMEM)
    layers, qlocal, lanes = q[0].shape
    sums = jax.ShapeDtypeStruct((qlocal, lanes), jnp.float32)
    return pl.pallas_call(
        start_kernel,
        out_shape=[jax.ShapeDtypeStruct((layers, lanes), jnp.float32), sums, sums],
        in_specs=[vmem] * (len(parts) + len(q)),
        out_specs=[vmem] * 3,
        compiler_params=pltpu.CompilerParams(vmem_limit_bytes=SMALL_VMEM),
        cost_estimate=NO_COST,
        name="score_start",
    )(*parts, *q)


def score_kernel(entries, factor_ref, unit_ref, dots_ref, squares_ref, q_ref, out_ref):
    dots, squares = add_blocks(dots_ref[...], squares_ref[...], unit_ref, q_ref)
    dots, squares = [jnp.sum(x.T, axis=0, keepdims=True) for x in (dots, squares)]
    scores = dots / jnp.sqrt(squares / entries + 1e-06)
    out_ref[...] = jnp.where(factor_ref[...] == 0.0, 0.0, scores * factor_ref[...])


def score(entries, factor, started, q):
    vmem = pl.BlockSpec(memory_space=pltpu.VMEM)
    return pl.pallas_call(
        functools.partial(score_kernel, entries),
        out_shape=jax.ShapeDtypeStruct((1, q.shape[1]), jnp.float32),
        in_specs=[vmem] * 5,
        out_specs=vmem,
        compiler_params=pltpu.CompilerParams(vmem_limit_bytes=SMALL_VMEM),
        cost_estimate=NO_COST,
        name="score",
    )(factor, *started, q)


def hops(k):
    return 2 if k == 2 else 1


def body(hidden_in, out_grad, proj_in, proj_out, token_mask, cand_ids, queries):
    rank = proj_in.shape[1]
    devices = lax.axis_size("tensor")
    chips = devices // 2
    dp = lax.axis_size("dp")
    me = lax.axis_index("tensor").astype(jnp.int32)
    core, chip = me % 2, me // 2
    qlocal, qcols = queries.shape

    def swap(x, mask):
        return lax.ppermute(x, "tensor", [(i, i ^ mask) for i in range(devices)])

    with jax.named_scope("gather_queries"):
        layers = dp // ROWS
        columns = [[z * ROWS + y for z in range(layers)] for y in range(ROWS)]
        copies = jnp.broadcast_to(queries[None], (layers, *queries.shape))
        column = lax.all_to_all(copies, "dp", 0, 0, tiled=True, axis_index_groups=columns)
        gathered = [column] + [lax.ppermute(column, "dp", [(i, i ^ k) for i in range(dp)]) for k in ROW_ORDER[1:]]

    with jax.named_scope("project"):
        theirs, kept = project_theirs(core, chip, hidden_in, out_grad, proj_in.T, proj_out.T)
        arrived = [swap(part, 1) for part in theirs]
        mine = project_mine(*kept)
    with jax.named_scope("exchange_tokens"):
        blocks = pair_sum(mine, arrived)
        order = sorted(range(1, chips), key=hops, reverse=True)
        parts = [blocks[0]] + [swap(blocks[k], 2 * k) for k in order]
    with jax.named_scope("outer"):
        row = lax.axis_index("dp").astype(jnp.int32) % ROWS
        partial = outer(core * chips + chip, row, token_mask.reshape(-1, BLOCK), parts)
    with jax.named_scope("exchange_grad"):
        pair = sum_parts([partial, swap(partial, 1)])
        four = sum_parts([pair, swap(pair, 2)])
        partials = [four, swap(four, 6)]
    with jax.named_scope("score"):
        index = me * qlocal + jnp.arange(qlocal, dtype=jnp.int32)
        factor = jnp.where(index[None, :] == cand_ids[:, None], jnp.float32(0.0), jnp.float32(1.0 / rank))
        return score(rank * rank, factor, score_start(partials, gathered[:-1]), gathered[-1])


def solution(mesh):
    placed = (
        P("dp", "tensor"),
        P("dp", "tensor"),
        P("tensor", None),
        P("tensor", None),
        P("dp"),
        P("dp"),
        P("tensor", "dp"),
    )
    return jax.shard_map(
        body, mesh=mesh, in_specs=placed, out_specs=P("dp", "tensor"), check_vma=False
    )
```

time: 40.2 us -> 38.6 us (0.960)
  Pallas kernels: 8.4 us -> 7.32 us
    pallas_call x1, Pallas kernels: 5.05 us -> 4.5 us  [project_theirs(): pl.pallas_call(functools.partial(theirs_kernel, n), out_shape=[jax.ShapeD...]
    pallas_call x3, Pallas kernels: 1.62 us -> 1.09 us  [the longest x1 0.7 us: score(): pl.pallas_call(functools.partial(score_kernel, entries), out_shape=jax.Sh...]
    ppermute x10 -> x8, starting transfers between devices: 8.87 us -> 8.44 us  [swap(): return lax.ppermute(x, 'tensor', [(i, i ^ mask) for i in range(devices)])]
    ppermute x10 -> x8, waiting for transfers between devices: 7.44 us -> 7.5 us  [swap(): return lax.ppermute(x, 'tensor', [(i, i ^ mask) for i in range(devices)])]
  transfers between devices with their start and end apart: 14 -> 12, of which waited for: 6 -> 6; matrix products, arithmetic and copies ran while one was open for 0% -> 0% of each run, Pallas kernels for 18% -> 17%
where the time goes in v1:
time: 38.6 us; the launch traced here: 38.3 us
  starting transfers between devices  21.3 us (55%)
  waiting for transfers between devices  7.51 us (19%)
  Pallas kernels  7.32 us (19%)
  local copies, waits for them, and re-layouts  1.49 us (4%)
  between operations  0.74 us (2%)
    all_to_all x1, starting transfers between devices, body(): lax.all_to_all(copies, 'dp', 0, 0, tiled=True, axis_index_groups=columns)  8.57 us
    ppermute x8, starting transfers between devices, swap(): return lax.ppermute(x, 'tensor', [(i, i ^ mask) for i in range(devices)])  8.44 us
    ppermute x8, waiting for transfers between devices, swap(): return lax.ppermute(x, 'tensor', [(i, i ^ mask) for i in range(devices)])  7.5 us
    pallas_call x1, Pallas kernels, project_theirs(): pl.pallas_call(functools.partial(theirs_kernel, n), out_shape=[jax.ShapeD...  4.5 us
    ppermute x3, starting transfers between devices, body(): lax.ppermute(column, 'dp', [(i, i ^ k) for i in range(dp)])  4.25 us
    broadcast_in_dim x1, local copies, waits for them, and re-layouts, body(): copies = jnp.broadcast_to(queries[None], (layers, *queries.shape))  1.48 us
    pallas_call x1, Pallas kernels, project_mine(): pl.pallas_call(mine_kernel, out_shape=[jax.ShapeDtypeStruct((BLOCK, w.sha...  1.36 us
  transfers between devices with their start and end apart: 12, of which 6 were waited for; matrix products, arithmetic and copies ran while one was open for 0% of the time, Pallas kernels for 17%

profile of v1, /device:TPU:56, one launch (start us, length us, event | category | flops | bytes accessed | tf_op | source)
XLA Modules:
  0.0 38.3 jit_solution(16184097936447179968)
XLA Ops:
  0.0 1.5 %broadcast_in_dim.34 = bf16[8,128,128]{2,1,0:T(8,128)(2,1)} broadcast(bf16[128,128]{1,0:T(8,128)(2,1)} %param.13), dimensions={1,2} | broadcast | bytes 294912 | tf_op jit(solution)/shard_map/gather_queries/broadcast_in_dim | solution.py:264
  1.5 8.6 %all-to-all-start = ((bf16[8,128,128]{2,1,0:T(8,128)(2,1)}), bf16[8,128,128]{2,1,0:T(8,128)(2,1)S(1)}, u32[]{:S(2)}, u32[]{:S(2)}) async-start(bf16[8,128,128]{2,1,0:T(8,128)(2,1)} %broadcast_in_dim.34), calls=%async_computation | async-start | bytes 524288 | tf_op jit(solution)/shard_map/gather_queries/all_to_all | solution.py:265
  10.1 4.5 %project_theirs.1 = (f32[512,128]{1,0:T(8,128)S(1)}, f32[512,128]{1,0:T(8,128)S(1)}, bf16[1024,1792]{1,0:T(8,128)(2,1)S(1)}, bf16[1024,512]{1,0:T(8,128)(2,1)S(1)}, bf16[128,2304]{1,0:T(8,128)(2,1)S(1)}) custom-call(s32[1]{0:T(128)} %bitcast.3.core_ref, s32[1]{0:T(128)} %bitcast.4.chip_ref, bf16[2048,1792]{1,0:T(8,128)(2,1)} %hidden_ref.1, ...), custom_call_target="tpu_custom_call" | custom-call | tf_op jit(solution)/shard_map/project/project_theirs/pallas_call | solution.py:75
  14.6 0.0 copy-start
  14.6 0.1 collective-permute-start
  14.7 0.5 %collective-permute-start.1 = (f32[512,128]{1,0:T(8,128)S(1)}, f32[512,128]{1,0:T(8,128)S(1)}, u32[]{:S(2)}, u32[]{:S(2)}) collective-permute-start(f32[512,128]{1,0:T(8,128)S(1)} %get-tuple-element.29), channel_id=1, source_target_pairs={{0,1},{1,0},{2,3},{3,2},{4,5},{5,4},{6,7},{7,6},{8,9},{9,8},{10,11... | collective-permute-start | bytes 786440 | tf_op jit(solution)/shard_map/project/ppermute | solution.py:259
  15.2 1.4 %project_mine.1 = (f32[256,128]{1,0:T(8,128)S(1)}, f32[256,128]{1,0:T(8,128)S(1)}, f32[256,128]{1,0:T(8,128)S(1)}, f32[256,128]{1,0:T(8,128)S(1)}) custom-call(bf16[1024,1792]{1,0:T(8,128)(2,1)S(1)} %get-tuple-element.21.hidden_ref, bf16[1024,512]{1,0:T(8,128)(2,1)S(1)} %get-tuple-element.22.grad_ref, bf16[128,2304]{1,0:T(8,128)(2,1)S(1)} %get-tuple-element.23.w_ref), custom_call_target="tpu_custom_call" | custom-call | tf_op jit(solution)/shard_map/project/project_mine/pallas_call | solution.py:108
  16.5 0.0 collective-permute-done.refs_4_
  16.6 0.0 collective-permute-done.1.refs_5_
  16.6 0.1 pair_sum.1
  16.6 3.1 %collective-permute-start.2 = (f32[256,128]{1,0:T(8,128)S(1)}, f32[256,128]{1,0:T(8,128)S(1)}, u32[]{:S(2)}, u32[]{:S(2)}) collective-permute-start(f32[256,128]{1,0:T(8,128)S(1)} %get-tuple-element.31), channel_id=1, source_target_pairs={{0,4},{1,5},{2,6},{3,7},{4,0},{5,1},{6,2},{7,3},{8,12},{9,13},{10,... | collective-permute-start | bytes 393224 | tf_op jit(solution)/shard_map/exchange_tokens/ppermute | solution.py:259
  19.7 0.6 %collective-permute-start.3 = (f32[256,128]{1,0:T(8,128)S(1)}, f32[256,128]{1,0:T(8,128)S(1)}, u32[]{:S(2)}, u32[]{:S(2)}) collective-permute-start(f32[256,128]{1,0:T(8,128)S(1)} %get-tuple-element.32), channel_id=1, source_target_pairs={{0,2},{1,3},{2,0},{3,1},{4,6},{5,7},{6,4},{7,5},{8,10},{9,11},{10,... | collective-permute-start | bytes 393224 | tf_op jit(solution)/shard_map/exchange_tokens/ppermute | solution.py:259
  20.3 0.6 %collective-permute-start.4 = (f32[256,128]{1,0:T(8,128)S(1)}, f32[256,128]{1,0:T(8,128)S(1)}, u32[]{:S(2)}, u32[]{:S(2)}) collective-permute-start(f32[256,128]{1,0:T(8,128)S(1)} %get-tuple-element.33), channel_id=1, source_target_pairs={{0,6},{1,7},{2,4},{3,5},{4,2},{5,3},{6,0},{7,1},{8,14},{9,15},{10,... | collective-permute-start | bytes 393224 | tf_op jit(solution)/shard_map/exchange_tokens/ppermute | solution.py:259
  20.9 0.0 all-to-all-done.refs_0_
  20.9 1.3 %collective-permute-start.8 = (bf16[8,128,128]{2,1,0:T(8,128)(2,1)S(1)}, bf16[8,128,128]{2,1,0:T(8,128)(2,1)S(1)}, u32[]{:S(2)}, u32[]{:S(2)}) collective-permute-start(bf16[8,128,128]{2,1,0:T(8,128)(2,1)S(1)} %all-to-all-done.refs_0_), channel_id=1, source_target_pairs={{0,16},{8,24},{16,0},{24,8},{32,48},{40,56},{48,32},{56,40},{64,80... | collective-permute-start | bytes 786440 | tf_op jit(solution)/shard_map/gather_queries/ppermute | solution.py:266
  22.2 2.2 %collective-permute-start.9 = (bf16[8,128,128]{2,1,0:T(8,128)(2,1)S(1)}, bf16[8,128,128]{2,1,0:T(8,128)(2,1)S(1)}, u32[]{:S(2)}, u32[]{:S(2)}) collective-permute-start(bf16[8,128,128]{2,1,0:T(8,128)(2,1)S(1)} %all-to-all-done.refs_0_), channel_id=1, source_target_pairs={{0,24},{8,16},{16,8},{24,0},{32,56},{40,48},{48,40},{56,32},{64,88... | collective-permute-start | bytes 786440 | tf_op jit(solution)/shard_map/gather_queries/ppermute | solution.py:266
  24.4 0.2 collective-permute-done.2.refs_1_
  24.6 0.7 %collective-permute-start.10 = (bf16[8,128,128]{2,1,0:T(8,128)(2,1)S(1)}, bf16[8,128,128]{2,1,0:T(8,128)(2,1)S(1)}, u32[]{:S(2)}, u32[]{:S(2)}) collective-permute-start(bf16[8,128,128]{2,1,0:T(8,128)(2,1)S(1)} %all-to-all-done.refs_0_), channel_id=1, source_target_pairs={{0,8},{8,0},{16,24},{24,16},{32,40},{40,32},{48,56},{56,48},{64,72... | collective-permute-start | bytes 786440 | tf_op jit(solution)/shard_map/gather_queries/ppermute | solution.py:266
  25.3 1.3 %collective-permute-done.3.refs_2_ = f32[256,128]{1,0:T(8,128)S(1)} collective-permute-done((f32[256,128]{1,0:T(8,128)S(1)}, f32[256,128]{1,0:T(8,128)S(1)}, u32[]{:S(2)}, u32[]{:S(2)}) %collective-permute-start.3) | collective-permute-done | bytes 131104 | tf_op jit(solution)/shard_map/exchange_tokens/ppermute | solution.py:259
  26.7 0.3 collective-permute-done.4.refs_3_
  26.9 0.4 outer.1.refs_0_
  27.3 0.1 collective-permute-start.5
  27.4 1.2 %collective-permute-done.5.refs_1_ = f32[32,128]{1,0:T(8,128)S(1)} collective-permute-done((f32[32,128]{1,0:T(8,128)S(1)}, f32[32,128]{1,0:T(8,128)S(1)}, u32[]{:S(2)}, u32[]{:S(2)}) %collective-permute-start.5) | collective-permute-done | bytes 16416 | tf_op jit(solution)/shard_map/exchange_grad/ppermute | solution.py:259
  28.6 1.1 %collective-permute-start.6 = (f32[32,128]{1,0:T(8,128)S(1)}, f32[32,128]{1,0:T(8,128)S(1)}, u32[]{:S(2)}, u32[]{:S(2)}) collective-permute-start(f32[32,128]{1,0:T(8,128)S(1)} %sum_parts.2.refs_0_), channel_id=1, source_target_pairs={{0,2},{1,3},{2,0},{3,1},{4,6},{5,7},{6,4},{7,5},{8,10},{9,11},{10,... | collective-permute-start | bytes 49160 | tf_op jit(solution)/shard_map/exchange_grad/ppermute | solution.py:259
  30.4 1.9 %collective-permute-done.6.refs_1_ = f32[32,128]{1,0:T(8,128)S(1)} collective-permute-done((f32[32,128]{1,0:T(8,128)S(1)}, f32[32,128]{1,0:T(8,128)S(1)}, u32[]{:S(2)}, u32[]{:S(2)}) %collective-permute-start.6) | collective-permute-done | bytes 16416 | tf_op jit(solution)/shard_map/exchange_grad/ppermute | solution.py:259
  32.3 2.4 %collective-permute-start.7 = (f32[32,128]{1,0:T(8,128)S(1)}, f32[32,128]{1,0:T(8,128)S(1)}, u32[]{:S(2)}, u32[]{:S(2)}) collective-permute-start(f32[32,128]{1,0:T(8,128)S(1)} %sum_parts.3.a_ref), channel_id=1, source_target_pairs={{0,6},{1,7},{2,4},{3,5},{4,2},{5,3},{6,0},{7,1},{8,14},{9,15},{10,... | collective-permute-start | bytes 49160 | tf_op jit(solution)/shard_map/exchange_grad/ppermute | solution.py:259
  34.7 2.6 %collective-permute-done.7.b_ref = f32[32,128]{1,0:T(8,128)S(1)} collective-permute-done((f32[32,128]{1,0:T(8,128)S(1)}, f32[32,128]{1,0:T(8,128)S(1)}, u32[]{:S(2)}, u32[]{:S(2)}) %collective-permute-start.7) | collective-permute-done | bytes 16416 | tf_op jit(solution)/shard_map/exchange_grad/ppermute | solution.py:259
  37.3 0.0 collective-permute-done.8.refs_1_
  37.3 0.0 collective-permute-done.9.refs_2_
  37.3 0.3 score_start.1
  37.6 0.0 collective-permute-done.10.q_ref
  37.6 0.7 %score.1 = f32[1,128]{1,0:T(1,128)} custom-call(f32[1,128]{1,0:T(1,128)S(1)} %compare_select_fusion.factor_ref, f32[8,128]{1,0:T(8,128)S(1)} %get-tuple-element.34.unit_ref, f32[128,128]{1,0:T(8,128)S(1)} %get-tuple-element.35.dots_ref, f32[128,128]{1,0:T(8,128)S(1)} %get-tuple-element.36.squares_ref, bf16[8,128,128]{2,1,0:T(8,128)(2,1)S(1)} %collective-permute-done.10.q_ref), custom_call_target="tpu_custom_call" | custom-call | tf_op jit(solution)/shard_map/score/score/pallas_call | solution.py:234
  (5 shorter events, 0.0 us)
Async XLA Ops:
  1.5 19.4 %all-to-all-start = ((bf16[8,128,128]{2,1,0:T(8,128)(2,1)}), bf16[8,128,128]{2,1,0:T(8,128)(2,1)S(1)}, u32[]{:S(2)}, u32[]{:S(2)}) async-start(bf16[8,128,128]{2,1,0:T(8,128)(2,1)} %broadcast_in_dim.34), calls=%async_computation | async-start | bytes 524288 | tf_op jit(solution)/shard_map/gather_queries/all_to_all | solution.py:265
  14.6 6.3 %copy-start = (s32[2048]{0:T(1024)S(1)}, s32[2048]{0:T(1024)}, u32[]{:S(2)}) copy-start(s32[2048]{0:T(1024)} %param.11) | copy-start | bytes 24580
  14.6 2.0 %collective-permute-start = (f32[512,128]{1,0:T(8,128)S(1)}, f32[512,128]{1,0:T(8,128)S(1)}, u32[]{:S(2)}, u32[]{:S(2)}) collective-permute-start(f32[512,128]{1,0:T(8,128)S(1)} %get-tuple-element.28), channel_id=1, source_target_pairs={{0,1},{1,0},{2,3},{3,2},{4,5},{5,4},{6,7},{7,6},{8,9},{9,8},{10,11... | collective-permute-start | bytes 786440 | tf_op jit(solution)/shard_map/project/ppermute | solution.py:259
  14.7 1.9 %collective-permute-start.1 = (f32[512,128]{1,0:T(8,128)S(1)}, f32[512,128]{1,0:T(8,128)S(1)}, u32[]{:S(2)}, u32[]{:S(2)}) collective-permute-start(f32[512,128]{1,0:T(8,128)S(1)} %get-tuple-element.29), channel_id=1, source_target_pairs={{0,1},{1,0},{2,3},{3,2},{4,5},{5,4},{6,7},{7,6},{8,9},{9,8},{10,11... | collective-permute-start | bytes 786440 | tf_op jit(solution)/shard_map/project/ppermute | solution.py:259
  16.6 7.9 %collective-permute-start.2 = (f32[256,128]{1,0:T(8,128)S(1)}, f32[256,128]{1,0:T(8,128)S(1)}, u32[]{:S(2)}, u32[]{:S(2)}) collective-permute-start(f32[256,128]{1,0:T(8,128)S(1)} %get-tuple-element.31), channel_id=1, source_target_pairs={{0,4},{1,5},{2,6},{3,7},{4,0},{5,1},{6,2},{7,3},{8,12},{9,13},{10,... | collective-permute-start | bytes 393224 | tf_op jit(solution)/shard_map/exchange_tokens/ppermute | solution.py:259
  19.7 6.9 %collective-permute-start.3 = (f32[256,128]{1,0:T(8,128)S(1)}, f32[256,128]{1,0:T(8,128)S(1)}, u32[]{:S(2)}, u32[]{:S(2)}) collective-permute-start(f32[256,128]{1,0:T(8,128)S(1)} %get-tuple-element.32), channel_id=1, source_target_pairs={{0,2},{1,3},{2,0},{3,1},{4,6},{5,7},{6,4},{7,5},{8,10},{9,11},{10,... | collective-permute-start | bytes 393224 | tf_op jit(solution)/shard_map/exchange_tokens/ppermute | solution.py:259
  20.3 6.6 %collective-permute-start.4 = (f32[256,128]{1,0:T(8,128)S(1)}, f32[256,128]{1,0:T(8,128)S(1)}, u32[]{:S(2)}, u32[]{:S(2)}) collective-permute-start(f32[256,128]{1,0:T(8,128)S(1)} %get-tuple-element.33), channel_id=1, source_target_pairs={{0,6},{1,7},{2,4},{3,5},{4,2},{5,3},{6,0},{7,1},{8,14},{9,15},{10,... | collective-permute-start | bytes 393224 | tf_op jit(solution)/shard_map/exchange_tokens/ppermute | solution.py:259
  20.9 16.4 %collective-permute-start.8 = (bf16[8,128,128]{2,1,0:T(8,128)(2,1)S(1)}, bf16[8,128,128]{2,1,0:T(8,128)(2,1)S(1)}, u32[]{:S(2)}, u32[]{:S(2)}) collective-permute-start(bf16[8,128,128]{2,1,0:T(8,128)(2,1)S(1)} %all-to-all-done.refs_0_), channel_id=1, source_target_pairs={{0,16},{8,24},{16,0},{24,8},{32,48},{40,56},{48,32},{56,40},{64,80... | collective-permute-start | bytes 786440 | tf_op jit(solution)/shard_map/gather_queries/ppermute | solution.py:266
  22.2 15.0 %collective-permute-start.9 = (bf16[8,128,128]{2,1,0:T(8,128)(2,1)S(1)}, bf16[8,128,128]{2,1,0:T(8,128)(2,1)S(1)}, u32[]{:S(2)}, u32[]{:S(2)}) collective-permute-start(bf16[8,128,128]{2,1,0:T(8,128)(2,1)S(1)} %all-to-all-done.refs_0_), channel_id=1, source_target_pairs={{0,24},{8,16},{16,8},{24,0},{32,56},{40,48},{48,40},{56,32},{64,88... | collective-permute-start | bytes 786440 | tf_op jit(solution)/shard_map/gather_queries/ppermute | solution.py:266
  24.6 13.0 %collective-permute-start.10 = (bf16[8,128,128]{2,1,0:T(8,128)(2,1)S(1)}, bf16[8,128,128]{2,1,0:T(8,128)(2,1)S(1)}, u32[]{:S(2)}, u32[]{:S(2)}) collective-permute-start(bf16[8,128,128]{2,1,0:T(8,128)(2,1)S(1)} %all-to-all-done.refs_0_), channel_id=1, source_target_pairs={{0,8},{8,0},{16,24},{24,16},{32,40},{40,32},{48,56},{56,48},{64,72... | collective-permute-start | bytes 786440 | tf_op jit(solution)/shard_map/gather_queries/ppermute | solution.py:266
  27.3 1.2 %collective-permute-start.5 = (f32[32,128]{1,0:T(8,128)S(1)}, f32[32,128]{1,0:T(8,128)S(1)}, u32[]{:S(2)}, u32[]{:S(2)}) collective-permute-start(f32[32,128]{1,0:T(8,128)S(1)} %outer.1.refs_0_), channel_id=1, source_target_pairs={{0,1},{1,0},{2,3},{3,2},{4,5},{5,4},{6,7},{7,6},{8,9},{9,8},{10,11... | collective-permute-start | bytes 49160 | tf_op jit(solution)/shard_map/exchange_grad/ppermute | solution.py:259
  28.6 3.7 %collective-permute-start.6 = (f32[32,128]{1,0:T(8,128)S(1)}, f32[32,128]{1,0:T(8,128)S(1)}, u32[]{:S(2)}, u32[]{:S(2)}) collective-permute-start(f32[32,128]{1,0:T(8,128)S(1)} %sum_parts.2.refs_0_), channel_id=1, source_target_pairs={{0,2},{1,3},{2,0},{3,1},{4,6},{5,7},{6,4},{7,5},{8,10},{9,11},{10,... | collective-permute-start | bytes 49160 | tf_op jit(solution)/shard_map/exchange_grad/ppermute | solution.py:259
  32.3 4.9 %collective-permute-start.7 = (f32[32,128]{1,0:T(8,128)S(1)}, f32[32,128]{1,0:T(8,128)S(1)}, u32[]{:S(2)}, u32[]{:S(2)}) collective-permute-start(f32[32,128]{1,0:T(8,128)S(1)} %sum_parts.3.a_ref), channel_id=1, source_target_pairs={{0,6},{1,7},{2,4},{3,5},{4,2},{5,3},{6,0},{7,1},{8,14},{9,15},{10,... | collective-permute-start | bytes 49160 | tf_op jit(solution)/shard_map/exchange_grad/ppermute | solution.py:259

commit v2 on v1

--- a/solution.py
+++ b/solution.py
@@ -271,15 +271,15 @@
         mine = project_mine(*kept)
     with jax.named_scope("exchange_tokens"):
         blocks = pair_sum(mine, arrived)
-        order = sorted(range(1, chips), key=hops, reverse=True)
+        order = sorted(range(1, chips), key=lambda k: (-hops(k), -k))
         parts = [blocks[0]] + [swap(blocks[k], 2 * k) for k in order]
     with jax.named_scope("outer"):
         row = lax.axis_index("dp").astype(jnp.int32) % ROWS
         partial = outer(core * chips + chip, row, token_mask.reshape(-1, BLOCK), parts)
     with jax.named_scope("exchange_grad"):
         pair = sum_parts([partial, swap(partial, 1)])
-        four = sum_parts([pair, swap(pair, 2)])
-        partials = [four, swap(four, 6)]
+        four = sum_parts([pair, swap(pair, 6)])
+        partials = [four, swap(four, 2)]
     with jax.named_scope("score"):
         index = me * qlocal + jnp.arange(qlocal, dtype=jnp.int32)
         factor = jnp.where(index[None, :] == cand_ids[:, None], jnp.float32(0.0), jnp.float32(1.0 / rank))

time: 38.6 us -> 38.3 us (level)
  starting transfers between devices: 21.3 us -> 20 us
  waiting for transfers between devices: 7.51 us -> 8.4 us
    ppermute x8, waiting for transfers between devices: 7.5 us -> 8.39 us  [swap(): return lax.ppermute(x, 'tensor', [(i, i ^ mask) for i in range(devices)])]
    ppermute x3, starting transfers between devices: 4.25 us -> 3.62 us  [body(): lax.ppermute(column, 'dp', [(i, i ^ k) for i in range(dp)])]
    ppermute x8, starting transfers between devices: 8.44 us -> 7.86 us  [swap(): return lax.ppermute(x, 'tensor', [(i, i ^ mask) for i in range(devices)])]
  transfers between devices with their start and end apart: 12 -> 12, of which waited for: 6 -> 5; matrix products, arithmetic and copies ran while one was open for 0% -> 0% of each run, Pallas kernels for 17% -> 17%
where the time goes in v2:
time: 38.3 us; the launch traced here: 38 us
  starting transfers between devices  20 us (52%)
  waiting for transfers between devices  8.4 us (22%)
  Pallas kernels  7.32 us (19%)
  local copies, waits for them, and re-layouts  1.49 us (4%)
  between operations  0.75 us (2%)
    all_to_all x1, starting transfers between devices, body(): lax.all_to_all(copies, 'dp', 0, 0, tiled=True, axis_index_groups=columns)  8.57 us
    ppermute x8, waiting for transfers between devices, swap(): return lax.ppermute(x, 'tensor', [(i, i ^ mask) for i in range(devices)])  8.39 us
    ppermute x8, starting transfers between devices, swap(): return lax.ppermute(x, 'tensor', [(i, i ^ mask) for i in range(devices)])  7.86 us
    pallas_call x1, Pallas kernels, project_theirs(): pl.pallas_call(functools.partial(theirs_kernel, n), out_shape=[jax.ShapeD...  4.5 us
    ppermute x3, starting transfers between devices, body(): lax.ppermute(column, 'dp', [(i, i ^ k) for i in range(dp)])  3.62 us
    broadcast_in_dim x1, local copies, waits for them, and re-layouts, body(): copies = jnp.broadcast_to(queries[None], (layers, *queries.shape))  1.48 us
    pallas_call x1, Pallas kernels, project_mine(): pl.pallas_call(mine_kernel, out_shape=[jax.ShapeDtypeStruct((BLOCK, w.sha...  1.36 us
  transfers between devices with their start and end apart: 12, of which 5 were waited for; matrix products, arithmetic and copies ran while one was open for 0% of the time, Pallas kernels for 17%

profile of v2, /device:TPU:56, one launch (start us, length us, event | category | flops | bytes accessed | tf_op | source)
XLA Modules:
  0.0 38.0 jit_solution(8008849317290119335)
XLA Ops:
  0.0 1.5 %broadcast_in_dim.34 = bf16[8,128,128]{2,1,0:T(8,128)(2,1)} broadcast(bf16[128,128]{1,0:T(8,128)(2,1)} %param.13), dimensions={1,2} | broadcast | bytes 294912 | tf_op jit(solution)/shard_map/gather_queries/broadcast_in_dim | solution.py:264
  1.5 8.6 %all-to-all-start = ((bf16[8,128,128]{2,1,0:T(8,128)(2,1)}), bf16[8,128,128]{2,1,0:T(8,128)(2,1)S(1)}, u32[]{:S(2)}, u32[]{:S(2)}) async-start(bf16[8,128,128]{2,1,0:T(8,128)(2,1)} %broadcast_in_dim.34), calls=%async_computation | async-start | bytes 524288 | tf_op jit(solution)/shard_map/gather_queries/all_to_all | solution.py:265
  10.1 4.5 %project_theirs.1 = (f32[512,128]{1,0:T(8,128)S(1)}, f32[512,128]{1,0:T(8,128)S(1)}, bf16[1024,1792]{1,0:T(8,128)(2,1)S(1)}, bf16[1024,512]{1,0:T(8,128)(2,1)S(1)}, bf16[128,2304]{1,0:T(8,128)(2,1)S(1)}) custom-call(s32[1]{0:T(128)} %bitcast.3.core_ref, s32[1]{0:T(128)} %bitcast.4.chip_ref, bf16[2048,1792]{1,0:T(8,128)(2,1)} %hidden_ref.1, ...), custom_call_target="tpu_custom_call" | custom-call | tf_op jit(solution)/shard_map/project/project_theirs/pallas_call | solution.py:75
  14.6 0.0 copy-start
  14.6 0.1 collective-permute-start
  14.7 0.5 %collective-permute-start.1 = (f32[512,128]{1,0:T(8,128)S(1)}, f32[512,128]{1,0:T(8,128)S(1)}, u32[]{:S(2)}, u32[]{:S(2)}) collective-permute-start(f32[512,128]{1,0:T(8,128)S(1)} %get-tuple-element.29), channel_id=1, source_target_pairs={{0,1},{1,0},{2,3},{3,2},{4,5},{5,4},{6,7},{7,6},{8,9},{9,8},{10,11... | collective-permute-start | bytes 786440 | tf_op jit(solution)/shard_map/project/ppermute | solution.py:259
  15.2 1.4 %project_mine.1 = (f32[256,128]{1,0:T(8,128)S(1)}, f32[256,128]{1,0:T(8,128)S(1)}, f32[256,128]{1,0:T(8,128)S(1)}, f32[256,128]{1,0:T(8,128)S(1)}) custom-call(bf16[1024,1792]{1,0:T(8,128)(2,1)S(1)} %get-tuple-element.21.hidden_ref, bf16[1024,512]{1,0:T(8,128)(2,1)S(1)} %get-tuple-element.22.grad_ref, bf16[128,2304]{1,0:T(8,128)(2,1)S(1)} %get-tuple-element.23.w_ref), custom_call_target="tpu_custom_call" | custom-call | tf_op jit(solution)/shard_map/project/project_mine/pallas_call | solution.py:108
  16.5 0.0 collective-permute-done.refs_4_
  16.6 0.0 collective-permute-done.1.refs_5_
  16.6 0.1 pair_sum.1
  16.6 3.1 %collective-permute-start.2 = (f32[256,128]{1,0:T(8,128)S(1)}, f32[256,128]{1,0:T(8,128)S(1)}, u32[]{:S(2)}, u32[]{:S(2)}) collective-permute-start(f32[256,128]{1,0:T(8,128)S(1)} %get-tuple-element.31), channel_id=1, source_target_pairs={{0,4},{1,5},{2,6},{3,7},{4,0},{5,1},{6,2},{7,3},{8,12},{9,13},{10,... | collective-permute-start | bytes 393224 | tf_op jit(solution)/shard_map/exchange_tokens/ppermute | solution.py:259
  19.7 1.1 %collective-permute-start.3 = (f32[256,128]{1,0:T(8,128)S(1)}, f32[256,128]{1,0:T(8,128)S(1)}, u32[]{:S(2)}, u32[]{:S(2)}) collective-permute-start(f32[256,128]{1,0:T(8,128)S(1)} %get-tuple-element.32), channel_id=1, source_target_pairs={{0,6},{1,7},{2,4},{3,5},{4,2},{5,3},{6,0},{7,1},{8,14},{9,15},{10,... | collective-permute-start | bytes 393224 | tf_op jit(solution)/shard_map/exchange_tokens/ppermute | solution.py:259
  20.9 0.0 collective-permute-start.4
  20.9 0.0 all-to-all-done.refs_0_
  20.9 1.3 %collective-permute-start.8 = (bf16[8,128,128]{2,1,0:T(8,128)(2,1)S(1)}, bf16[8,128,128]{2,1,0:T(8,128)(2,1)S(1)}, u32[]{:S(2)}, u32[]{:S(2)}) collective-permute-start(bf16[8,128,128]{2,1,0:T(8,128)(2,1)S(1)} %all-to-all-done.refs_0_), channel_id=1, source_target_pairs={{0,16},{8,24},{16,0},{24,8},{32,48},{40,56},{48,32},{56,40},{64,80... | collective-permute-start | bytes 786440 | tf_op jit(solution)/shard_map/gather_queries/ppermute | solution.py:266
  22.2 2.2 %collective-permute-start.9 = (bf16[8,128,128]{2,1,0:T(8,128)(2,1)S(1)}, bf16[8,128,128]{2,1,0:T(8,128)(2,1)S(1)}, u32[]{:S(2)}, u32[]{:S(2)}) collective-permute-start(bf16[8,128,128]{2,1,0:T(8,128)(2,1)S(1)} %all-to-all-done.refs_0_), channel_id=1, source_target_pairs={{0,24},{8,16},{16,8},{24,0},{32,56},{40,48},{48,40},{56,32},{64,88... | collective-permute-start | bytes 786440 | tf_op jit(solution)/shard_map/gather_queries/ppermute | solution.py:266
  24.4 0.0 collective-permute-done.2.refs_1_
  24.4 0.1 collective-permute-start.10
  24.5 2.0 %collective-permute-done.3.refs_2_ = f32[256,128]{1,0:T(8,128)S(1)} collective-permute-done((f32[256,128]{1,0:T(8,128)S(1)}, f32[256,128]{1,0:T(8,128)S(1)}, u32[]{:S(2)}, u32[]{:S(2)}) %collective-permute-start.3) | collective-permute-done | bytes 131104 | tf_op jit(solution)/shard_map/exchange_tokens/ppermute | solution.py:259
  26.6 0.1 collective-permute-done.4.refs_3_
  26.7 0.4 outer.1.refs_0_
  27.0 0.1 collective-permute-start.5
  27.1 1.2 %collective-permute-done.5.refs_1_ = f32[32,128]{1,0:T(8,128)S(1)} collective-permute-done((f32[32,128]{1,0:T(8,128)S(1)}, f32[32,128]{1,0:T(8,128)S(1)}, u32[]{:S(2)}, u32[]{:S(2)}) %collective-permute-start.5) | collective-permute-done | bytes 16416 | tf_op jit(solution)/shard_map/exchange_grad/ppermute | solution.py:259
  28.3 2.7 %collective-permute-start.6 = (f32[32,128]{1,0:T(8,128)S(1)}, f32[32,128]{1,0:T(8,128)S(1)}, u32[]{:S(2)}, u32[]{:S(2)}) collective-permute-start(f32[32,128]{1,0:T(8,128)S(1)} %sum_parts.2.refs_0_), channel_id=1, source_target_pairs={{0,6},{1,7},{2,4},{3,5},{4,2},{5,3},{6,0},{7,1},{8,14},{9,15},{10,... | collective-permute-start | bytes 49160 | tf_op jit(solution)/shard_map/exchange_grad/ppermute | solution.py:259
  31.6 1.6 %collective-permute-done.6.refs_1_ = f32[32,128]{1,0:T(8,128)S(1)} collective-permute-done((f32[32,128]{1,0:T(8,128)S(1)}, f32[32,128]{1,0:T(8,128)S(1)}, u32[]{:S(2)}, u32[]{:S(2)}) %collective-permute-start.6) | collective-permute-done | bytes 16416 | tf_op jit(solution)/shard_map/exchange_grad/ppermute | solution.py:259
  33.2 0.3 collective-permute-start.7
  33.5 3.5 %collective-permute-done.7.b_ref = f32[32,128]{1,0:T(8,128)S(1)} collective-permute-done((f32[32,128]{1,0:T(8,128)S(1)}, f32[32,128]{1,0:T(8,128)S(1)}, u32[]{:S(2)}, u32[]{:S(2)}) %collective-permute-start.7) | collective-permute-done | bytes 16416 | tf_op jit(solution)/shard_map/exchange_grad/ppermute | solution.py:259
  37.0 0.0 collective-permute-done.8.refs_1_
  37.0 0.0 collective-permute-done.9.refs_2_
  37.0 0.3 score_start.1
  37.3 0.0 collective-permute-done.10.q_ref
  37.3 0.7 %score.1 = f32[1,128]{1,0:T(1,128)} custom-call(f32[1,128]{1,0:T(1,128)S(1)} %compare_select_fusion.factor_ref, f32[8,128]{1,0:T(8,128)S(1)} %get-tuple-element.34.unit_ref, f32[128,128]{1,0:T(8,128)S(1)} %get-tuple-element.35.dots_ref, f32[128,128]{1,0:T(8,128)S(1)} %get-tuple-element.36.squares_ref, bf16[8,128,128]{2,1,0:T(8,128)(2,1)S(1)} %collective-permute-done.10.q_ref), custom_call_target="tpu_custom_call" | custom-call | tf_op jit(solution)/shard_map/score/score/pallas_call | solution.py:234
  (5 shorter events, 0.0 us)
Async XLA Ops:
  1.5 19.4 %all-to-all-start = ((bf16[8,128,128]{2,1,0:T(8,128)(2,1)}), bf16[8,128,128]{2,1,0:T(8,128)(2,1)S(1)}, u32[]{:S(2)}, u32[]{:S(2)}) async-start(bf16[8,128,128]{2,1,0:T(8,128)(2,1)} %broadcast_in_dim.34), calls=%async_computation | async-start | bytes 524288 | tf_op jit(solution)/shard_map/gather_queries/all_to_all | solution.py:265
  14.6 6.3 %copy-start = (s32[2048]{0:T(1024)S(1)}, s32[2048]{0:T(1024)}, u32[]{:S(2)}) copy-start(s32[2048]{0:T(1024)} %param.11) | copy-start | bytes 24580
  14.6 2.0 %collective-permute-start = (f32[512,128]{1,0:T(8,128)S(1)}, f32[512,128]{1,0:T(8,128)S(1)}, u32[]{:S(2)}, u32[]{:S(2)}) collective-permute-start(f32[512,128]{1,0:T(8,128)S(1)} %get-tuple-element.28), channel_id=1, source_target_pairs={{0,1},{1,0},{2,3},{3,2},{4,5},{5,4},{6,7},{7,6},{8,9},{9,8},{10,11... | collective-permute-start | bytes 786440 | tf_op jit(solution)/shard_map/project/ppermute | solution.py:259
  14.7 1.9 %collective-permute-start.1 = (f32[512,128]{1,0:T(8,128)S(1)}, f32[512,128]{1,0:T(8,128)S(1)}, u32[]{:S(2)}, u32[]{:S(2)}) collective-permute-start(f32[512,128]{1,0:T(8,128)S(1)} %get-tuple-element.29), channel_id=1, source_target_pairs={{0,1},{1,0},{2,3},{3,2},{4,5},{5,4},{6,7},{7,6},{8,9},{9,8},{10,11... | collective-permute-start | bytes 786440 | tf_op jit(solution)/shard_map/project/ppermute | solution.py:259
  16.6 7.8 %collective-permute-start.2 = (f32[256,128]{1,0:T(8,128)S(1)}, f32[256,128]{1,0:T(8,128)S(1)}, u32[]{:S(2)}, u32[]{:S(2)}) collective-permute-start(f32[256,128]{1,0:T(8,128)S(1)} %get-tuple-element.31), channel_id=1, source_target_pairs={{0,4},{1,5},{2,6},{3,7},{4,0},{5,1},{6,2},{7,3},{8,12},{9,13},{10,... | collective-permute-start | bytes 393224 | tf_op jit(solution)/shard_map/exchange_tokens/ppermute | solution.py:259
  19.7 6.8 %collective-permute-start.3 = (f32[256,128]{1,0:T(8,128)S(1)}, f32[256,128]{1,0:T(8,128)S(1)}, u32[]{:S(2)}, u32[]{:S(2)}) collective-permute-start(f32[256,128]{1,0:T(8,128)S(1)} %get-tuple-element.32), channel_id=1, source_target_pairs={{0,6},{1,7},{2,4},{3,5},{4,2},{5,3},{6,0},{7,1},{8,14},{9,15},{10,... | collective-permute-start | bytes 393224 | tf_op jit(solution)/shard_map/exchange_tokens/ppermute | solution.py:259
  20.9 5.8 %collective-permute-start.4 = (f32[256,128]{1,0:T(8,128)S(1)}, f32[256,128]{1,0:T(8,128)S(1)}, u32[]{:S(2)}, u32[]{:S(2)}) collective-permute-start(f32[256,128]{1,0:T(8,128)S(1)} %get-tuple-element.33), channel_id=1, source_target_pairs={{0,2},{1,3},{2,0},{3,1},{4,6},{5,7},{6,4},{7,5},{8,10},{9,11},{10,... | collective-permute-start | bytes 393224 | tf_op jit(solution)/shard_map/exchange_tokens/ppermute | solution.py:259
  20.9 16.0 %collective-permute-start.8 = (bf16[8,128,128]{2,1,0:T(8,128)(2,1)S(1)}, bf16[8,128,128]{2,1,0:T(8,128)(2,1)S(1)}, u32[]{:S(2)}, u32[]{:S(2)}) collective-permute-start(bf16[8,128,128]{2,1,0:T(8,128)(2,1)S(1)} %all-to-all-done.refs_0_), channel_id=1, source_target_pairs={{0,16},{8,24},{16,0},{24,8},{32,48},{40,56},{48,32},{56,40},{64,80... | collective-permute-start | bytes 786440 | tf_op jit(solution)/shard_map/gather_queries/ppermute | solution.py:266
  22.2 14.7 %collective-permute-start.9 = (bf16[8,128,128]{2,1,0:T(8,128)(2,1)S(1)}, bf16[8,128,128]{2,1,0:T(8,128)(2,1)S(1)}, u32[]{:S(2)}, u32[]{:S(2)}) collective-permute-start(bf16[8,128,128]{2,1,0:T(8,128)(2,1)S(1)} %all-to-all-done.refs_0_), channel_id=1, source_target_pairs={{0,24},{8,16},{16,8},{24,0},{32,56},{40,48},{48,40},{56,32},{64,88... | collective-permute-start | bytes 786440 | tf_op jit(solution)/shard_map/gather_queries/ppermute | solution.py:266
  24.4 12.9 %collective-permute-start.10 = (bf16[8,128,128]{2,1,0:T(8,128)(2,1)S(1)}, bf16[8,128,128]{2,1,0:T(8,128)(2,1)S(1)}, u32[]{:S(2)}, u32[]{:S(2)}) collective-permute-start(bf16[8,128,128]{2,1,0:T(8,128)(2,1)S(1)} %all-to-all-done.refs_0_), channel_id=1, source_target_pairs={{0,8},{8,0},{16,24},{24,16},{32,40},{40,32},{48,56},{56,48},{64,72... | collective-permute-start | bytes 786440 | tf_op jit(solution)/shard_map/gather_queries/ppermute | solution.py:266
  27.0 1.2 %collective-permute-start.5 = (f32[32,128]{1,0:T(8,128)S(1)}, f32[32,128]{1,0:T(8,128)S(1)}, u32[]{:S(2)}, u32[]{:S(2)}) collective-permute-start(f32[32,128]{1,0:T(8,128)S(1)} %outer.1.refs_0_), channel_id=1, source_target_pairs={{0,1},{1,0},{2,3},{3,2},{4,5},{5,4},{6,7},{7,6},{8,9},{9,8},{10,11... | collective-permute-start | bytes 49160 | tf_op jit(solution)/shard_map/exchange_grad/ppermute | solution.py:259
  28.3 4.9 %collective-permute-start.6 = (f32[32,128]{1,0:T(8,128)S(1)}, f32[32,128]{1,0:T(8,128)S(1)}, u32[]{:S(2)}, u32[]{:S(2)}) collective-permute-start(f32[32,128]{1,0:T(8,128)S(1)} %sum_parts.2.refs_0_), channel_id=1, source_target_pairs={{0,6},{1,7},{2,4},{3,5},{4,2},{5,3},{6,0},{7,1},{8,14},{9,15},{10,... | collective-permute-start | bytes 49160 | tf_op jit(solution)/shard_map/exchange_grad/ppermute | solution.py:259
  33.2 3.7 %collective-permute-start.7 = (f32[32,128]{1,0:T(8,128)S(1)}, f32[32,128]{1,0:T(8,128)S(1)}, u32[]{:S(2)}, u32[]{:S(2)}) collective-permute-start(f32[32,128]{1,0:T(8,128)S(1)} %sum_parts.3.a_ref), channel_id=1, source_target_pairs={{0,2},{1,3},{2,0},{3,1},{4,6},{5,7},{6,4},{7,5},{8,10},{9,11},{10,... | collective-permute-start | bytes 49160 | tf_op jit(solution)/shard_map/exchange_grad/ppermute | solution.py:259

commit v3 on v2

--- a/solution.py
+++ b/solution.py
@@ -141,12 +141,12 @@
     total = functools.reduce(lambda a, b: a + b, [r[...] for r in parts])
     rank = total.shape[1] // 2
     masked = total.T[rank:, :] * mask
-    tmp_ref[...] = lax.dot_general(
+    tmp_ref[:rank, :] = lax.dot_general(
         masked, total, (((1,), (0,)), ((), ())), preferred_element_type=jnp.float32, precision=HIGHEST
     )
     even = tmp_ref[pl.ds(0, rank // 2, stride=2), :]
     odd = tmp_ref[pl.ds(1, rank // 2, stride=2), :]
-    both_ref[...] = jnp.concatenate([even[:, :rank], odd[:, :rank]], axis=1)
+    both_ref[: rank // 2, :] = jnp.concatenate([even[:, :rank], odd[:, :rank]], axis=1)
     layers = out_ref.shape[0] // ROWS
     for k, other in enumerate(ROW_ORDER):
         row = jnp.bitwise_xor(row_ref[0], other)
@@ -161,7 +161,7 @@
         out_shape=jax.ShapeDtypeStruct((rank // 2, 2 * rank), jnp.float32),
         in_specs=[pl.BlockSpec(memory_space=pltpu.SMEM)] * 2 + [vmem] * (1 + len(parts)),
         out_specs=vmem,
-        scratch_shapes=[pltpu.VMEM((rank, 2 * rank), jnp.float32), pltpu.VMEM((rank // 2, 2 * rank), jnp.float32)],
+        scratch_shapes=[pltpu.VMEM((n + 8, 2 * rank), jnp.float32) for n in (rank, rank // 2)],
         compiler_params=pltpu.CompilerParams(vmem_limit_bytes=SMALL_VMEM),
         cost_estimate=pl.CostEstimate(flops=OUTER_FLOPS, bytes_accessed=0, transcendentals=0),
         name="outer",

time: 38.3 us -> 38.3 us (level)
  no operation moved by 1% of the time
where the time goes in v3:
time: 38.3 us; the launch traced here: 38 us
  starting transfers between devices  20 us (52%)
  waiting for transfers between devices  8.4 us (22%)
  Pallas kernels  7.32 us (19%)
  local copies, waits for them, and re-layouts  1.49 us (4%)
  between operations  0.75 us (2%)
    all_to_all x1, starting transfers between devices, body(): lax.all_to_all(copies, 'dp', 0, 0, tiled=True, axis_index_groups=columns)  8.57 us
    ppermute x8, waiting for transfers between devices, swap(): return lax.ppermute(x, 'tensor', [(i, i ^ mask) for i in range(devices)])  8.39 us
    ppermute x8, starting transfers between devices, swap(): return lax.ppermute(x, 'tensor', [(i, i ^ mask) for i in range(devices)])  7.86 us
    pallas_call x1, Pallas kernels, project_theirs(): pl.pallas_call(functools.partial(theirs_kernel, n), out_shape=[jax.ShapeD...  4.5 us
    ppermute x3, starting transfers between devices, body(): lax.ppermute(column, 'dp', [(i, i ^ k) for i in range(dp)])  3.62 us
    broadcast_in_dim x1, local copies, waits for them, and re-layouts, body(): copies = jnp.broadcast_to(queries[None], (layers, *queries.shape))  1.48 us
    pallas_call x1, Pallas kernels, project_mine(): pl.pallas_call(mine_kernel, out_shape=[jax.ShapeDtypeStruct((BLOCK, w.sha...  1.36 us
  transfers between devices with their start and end apart: 12, of which 5 were waited for; matrix products, arithmetic and copies ran while one was open for 0% of the time, Pallas kernels for 17%

profile of v3, /device:TPU:56, one launch (start us, length us, event | category | flops | bytes accessed | tf_op | source)
XLA Modules:
  0.0 38.0 jit_solution(4051120615519890819)
XLA Ops:
  0.0 1.5 %broadcast_in_dim.34 = bf16[8,128,128]{2,1,0:T(8,128)(2,1)} broadcast(bf16[128,128]{1,0:T(8,128)(2,1)} %param.13), dimensions={1,2} | broadcast | bytes 294912 | tf_op jit(solution)/shard_map/gather_queries/broadcast_in_dim | solution.py:264
  1.5 8.6 %all-to-all-start = ((bf16[8,128,128]{2,1,0:T(8,128)(2,1)}), bf16[8,128,128]{2,1,0:T(8,128)(2,1)S(1)}, u32[]{:S(2)}, u32[]{:S(2)}) async-start(bf16[8,128,128]{2,1,0:T(8,128)(2,1)} %broadcast_in_dim.34), calls=%async_computation | async-start | bytes 524288 | tf_op jit(solution)/shard_map/gather_queries/all_to_all | solution.py:265
  10.1 4.5 %project_theirs.1 = (f32[512,128]{1,0:T(8,128)S(1)}, f32[512,128]{1,0:T(8,128)S(1)}, bf16[1024,1792]{1,0:T(8,128)(2,1)S(1)}, bf16[1024,512]{1,0:T(8,128)(2,1)S(1)}, bf16[128,2304]{1,0:T(8,128)(2,1)S(1)}) custom-call(s32[1]{0:T(128)} %bitcast.3.core_ref, s32[1]{0:T(128)} %bitcast.4.chip_ref, bf16[2048,1792]{1,0:T(8,128)(2,1)} %hidden_ref.1, ...), custom_call_target="tpu_custom_call" | custom-call | tf_op jit(solution)/shard_map/project/project_theirs/pallas_call | solution.py:75
  14.6 0.0 copy-start
  14.6 0.1 collective-permute-start
  14.7 0.5 %collective-permute-start.1 = (f32[512,128]{1,0:T(8,128)S(1)}, f32[512,128]{1,0:T(8,128)S(1)}, u32[]{:S(2)}, u32[]{:S(2)}) collective-permute-start(f32[512,128]{1,0:T(8,128)S(1)} %get-tuple-element.29), channel_id=1, source_target_pairs={{0,1},{1,0},{2,3},{3,2},{4,5},{5,4},{6,7},{7,6},{8,9},{9,8},{10,11... | collective-permute-start | bytes 786440 | tf_op jit(solution)/shard_map/project/ppermute | solution.py:259
  15.2 1.4 %project_mine.1 = (f32[256,128]{1,0:T(8,128)S(1)}, f32[256,128]{1,0:T(8,128)S(1)}, f32[256,128]{1,0:T(8,128)S(1)}, f32[256,128]{1,0:T(8,128)S(1)}) custom-call(bf16[1024,1792]{1,0:T(8,128)(2,1)S(1)} %get-tuple-element.21.hidden_ref, bf16[1024,512]{1,0:T(8,128)(2,1)S(1)} %get-tuple-element.22.grad_ref, bf16[128,2304]{1,0:T(8,128)(2,1)S(1)} %get-tuple-element.23.w_ref), custom_call_target="tpu_custom_call" | custom-call | tf_op jit(solution)/shard_map/project/project_mine/pallas_call | solution.py:108
  16.5 0.0 collective-permute-done.refs_4_
  16.6 0.0 collective-permute-done.1.refs_5_
  16.6 0.1 pair_sum.1
  16.6 3.1 %collective-permute-start.2 = (f32[256,128]{1,0:T(8,128)S(1)}, f32[256,128]{1,0:T(8,128)S(1)}, u32[]{:S(2)}, u32[]{:S(2)}) collective-permute-start(f32[256,128]{1,0:T(8,128)S(1)} %get-tuple-element.31), channel_id=1, source_target_pairs={{0,4},{1,5},{2,6},{3,7},{4,0},{5,1},{6,2},{7,3},{8,12},{9,13},{10,... | collective-permute-start | bytes 393224 | tf_op jit(solution)/shard_map/exchange_tokens/ppermute | solution.py:259
  19.7 1.1 %collective-permute-start.3 = (f32[256,128]{1,0:T(8,128)S(1)}, f32[256,128]{1,0:T(8,128)S(1)}, u32[]{:S(2)}, u32[]{:S(2)}) collective-permute-start(f32[256,128]{1,0:T(8,128)S(1)} %get-tuple-element.32), channel_id=1, source_target_pairs={{0,6},{1,7},{2,4},{3,5},{4,2},{5,3},{6,0},{7,1},{8,14},{9,15},{10,... | collective-permute-start | bytes 393224 | tf_op jit(solution)/shard_map/exchange_tokens/ppermute | solution.py:259
  20.9 0.0 collective-permute-start.4
  20.9 0.0 all-to-all-done.refs_0_
  20.9 1.3 %collective-permute-start.8 = (bf16[8,128,128]{2,1,0:T(8,128)(2,1)S(1)}, bf16[8,128,128]{2,1,0:T(8,128)(2,1)S(1)}, u32[]{:S(2)}, u32[]{:S(2)}) collective-permute-start(bf16[8,128,128]{2,1,0:T(8,128)(2,1)S(1)} %all-to-all-done.refs_0_), channel_id=1, source_target_pairs={{0,16},{8,24},{16,0},{24,8},{32,48},{40,56},{48,32},{56,40},{64,80... | collective-permute-start | bytes 786440 | tf_op jit(solution)/shard_map/gather_queries/ppermute | solution.py:266
  22.2 2.2 %collective-permute-start.9 = (bf16[8,128,128]{2,1,0:T(8,128)(2,1)S(1)}, bf16[8,128,128]{2,1,0:T(8,128)(2,1)S(1)}, u32[]{:S(2)}, u32[]{:S(2)}) collective-permute-start(bf16[8,128,128]{2,1,0:T(8,128)(2,1)S(1)} %all-to-all-done.refs_0_), channel_id=1, source_target_pairs={{0,24},{8,16},{16,8},{24,0},{32,56},{40,48},{48,40},{56,32},{64,88... | collective-permute-start | bytes 786440 | tf_op jit(solution)/shard_map/gather_queries/ppermute | solution.py:266
  24.4 0.0 collective-permute-done.2.refs_1_
  24.4 0.1 collective-permute-start.10
  24.5 2.0 %collective-permute-done.3.refs_2_ = f32[256,128]{1,0:T(8,128)S(1)} collective-permute-done((f32[256,128]{1,0:T(8,128)S(1)}, f32[256,128]{1,0:T(8,128)S(1)}, u32[]{:S(2)}, u32[]{:S(2)}) %collective-permute-start.3) | collective-permute-done | bytes 131104 | tf_op jit(solution)/shard_map/exchange_tokens/ppermute | solution.py:259
  26.6 0.1 collective-permute-done.4.refs_3_
  26.7 0.4 outer.1.refs_0_
  27.0 0.1 collective-permute-start.5
  27.1 1.2 %collective-permute-done.5.refs_1_ = f32[32,128]{1,0:T(8,128)S(1)} collective-permute-done((f32[32,128]{1,0:T(8,128)S(1)}, f32[32,128]{1,0:T(8,128)S(1)}, u32[]{:S(2)}, u32[]{:S(2)}) %collective-permute-start.5) | collective-permute-done | bytes 16416 | tf_op jit(solution)/shard_map/exchange_grad/ppermute | solution.py:259
  28.3 2.7 %collective-permute-start.6 = (f32[32,128]{1,0:T(8,128)S(1)}, f32[32,128]{1,0:T(8,128)S(1)}, u32[]{:S(2)}, u32[]{:S(2)}) collective-permute-start(f32[32,128]{1,0:T(8,128)S(1)} %sum_parts.2.refs_0_), channel_id=1, source_target_pairs={{0,6},{1,7},{2,4},{3,5},{4,2},{5,3},{6,0},{7,1},{8,14},{9,15},{10,... | collective-permute-start | bytes 49160 | tf_op jit(solution)/shard_map/exchange_grad/ppermute | solution.py:259
  31.6 1.6 %collective-permute-done.6.refs_1_ = f32[32,128]{1,0:T(8,128)S(1)} collective-permute-done((f32[32,128]{1,0:T(8,128)S(1)}, f32[32,128]{1,0:T(8,128)S(1)}, u32[]{:S(2)}, u32[]{:S(2)}) %collective-permute-start.6) | collective-permute-done | bytes 16416 | tf_op jit(solution)/shard_map/exchange_grad/ppermute | solution.py:259
  33.2 0.3 collective-permute-start.7
  33.5 3.5 %collective-permute-done.7.b_ref = f32[32,128]{1,0:T(8,128)S(1)} collective-permute-done((f32[32,128]{1,0:T(8,128)S(1)}, f32[32,128]{1,0:T(8,128)S(1)}, u32[]{:S(2)}, u32[]{:S(2)}) %collective-permute-start.7) | collective-permute-done | bytes 16416 | tf_op jit(solution)/shard_map/exchange_grad/ppermute | solution.py:259
  37.0 0.0 collective-permute-done.8.refs_1_
  37.0 0.0 collective-permute-done.9.refs_2_
  37.0 0.3 score_start.1
  37.3 0.0 collective-permute-done.10.q_ref
  37.3 0.7 %score.1 = f32[1,128]{1,0:T(1,128)} custom-call(f32[1,128]{1,0:T(1,128)S(1)} %compare_select_fusion.factor_ref, f32[8,128]{1,0:T(8,128)S(1)} %get-tuple-element.34.unit_ref, f32[128,128]{1,0:T(8,128)S(1)} %get-tuple-element.35.dots_ref, f32[128,128]{1,0:T(8,128)S(1)} %get-tuple-element.36.squares_ref, bf16[8,128,128]{2,1,0:T(8,128)(2,1)S(1)} %collective-permute-done.10.q_ref), custom_call_target="tpu_custom_call" | custom-call | tf_op jit(solution)/shard_map/score/score/pallas_call | solution.py:234
  (5 shorter events, 0.0 us)
Async XLA Ops:
  1.5 19.4 %all-to-all-start = ((bf16[8,128,128]{2,1,0:T(8,128)(2,1)}), bf16[8,128,128]{2,1,0:T(8,128)(2,1)S(1)}, u32[]{:S(2)}, u32[]{:S(2)}) async-start(bf16[8,128,128]{2,1,0:T(8,128)(2,1)} %broadcast_in_dim.34), calls=%async_computation | async-start | bytes 524288 | tf_op jit(solution)/shard_map/gather_queries/all_to_all | solution.py:265
  14.6 6.3 %copy-start = (s32[2048]{0:T(1024)S(1)}, s32[2048]{0:T(1024)}, u32[]{:S(2)}) copy-start(s32[2048]{0:T(1024)} %param.11) | copy-start | bytes 24580
  14.6 2.0 %collective-permute-start = (f32[512,128]{1,0:T(8,128)S(1)}, f32[512,128]{1,0:T(8,128)S(1)}, u32[]{:S(2)}, u32[]{:S(2)}) collective-permute-start(f32[512,128]{1,0:T(8,128)S(1)} %get-tuple-element.28), channel_id=1, source_target_pairs={{0,1},{1,0},{2,3},{3,2},{4,5},{5,4},{6,7},{7,6},{8,9},{9,8},{10,11... | collective-permute-start | bytes 786440 | tf_op jit(solution)/shard_map/project/ppermute | solution.py:259
  14.7 1.9 %collective-permute-start.1 = (f32[512,128]{1,0:T(8,128)S(1)}, f32[512,128]{1,0:T(8,128)S(1)}, u32[]{:S(2)}, u32[]{:S(2)}) collective-permute-start(f32[512,128]{1,0:T(8,128)S(1)} %get-tuple-element.29), channel_id=1, source_target_pairs={{0,1},{1,0},{2,3},{3,2},{4,5},{5,4},{6,7},{7,6},{8,9},{9,8},{10,11... | collective-permute-start | bytes 786440 | tf_op jit(solution)/shard_map/project/ppermute | solution.py:259
  16.6 7.8 %collective-permute-start.2 = (f32[256,128]{1,0:T(8,128)S(1)}, f32[256,128]{1,0:T(8,128)S(1)}, u32[]{:S(2)}, u32[]{:S(2)}) collective-permute-start(f32[256,128]{1,0:T(8,128)S(1)} %get-tuple-element.31), channel_id=1, source_target_pairs={{0,4},{1,5},{2,6},{3,7},{4,0},{5,1},{6,2},{7,3},{8,12},{9,13},{10,... | collective-permute-start | bytes 393224 | tf_op jit(solution)/shard_map/exchange_tokens/ppermute | solution.py:259
  19.7 6.8 %collective-permute-start.3 = (f32[256,128]{1,0:T(8,128)S(1)}, f32[256,128]{1,0:T(8,128)S(1)}, u32[]{:S(2)}, u32[]{:S(2)}) collective-permute-start(f32[256,128]{1,0:T(8,128)S(1)} %get-tuple-element.32), channel_id=1, source_target_pairs={{0,6},{1,7},{2,4},{3,5},{4,2},{5,3},{6,0},{7,1},{8,14},{9,15},{10,... | collective-permute-start | bytes 393224 | tf_op jit(solution)/shard_map/exchange_tokens/ppermute | solution.py:259
  20.9 5.8 %collective-permute-start.4 = (f32[256,128]{1,0:T(8,128)S(1)}, f32[256,128]{1,0:T(8,128)S(1)}, u32[]{:S(2)}, u32[]{:S(2)}) collective-permute-start(f32[256,128]{1,0:T(8,128)S(1)} %get-tuple-element.33), channel_id=1, source_target_pairs={{0,2},{1,3},{2,0},{3,1},{4,6},{5,7},{6,4},{7,5},{8,10},{9,11},{10,... | collective-permute-start | bytes 393224 | tf_op jit(solution)/shard_map/exchange_tokens/ppermute | solution.py:259
  20.9 16.0 %collective-permute-start.8 = (bf16[8,128,128]{2,1,0:T(8,128)(2,1)S(1)}, bf16[8,128,128]{2,1,0:T(8,128)(2,1)S(1)}, u32[]{:S(2)}, u32[]{:S(2)}) collective-permute-start(bf16[8,128,128]{2,1,0:T(8,128)(2,1)S(1)} %all-to-all-done.refs_0_), channel_id=1, source_target_pairs={{0,16},{8,24},{16,0},{24,8},{32,48},{40,56},{48,32},{56,40},{64,80... | collective-permute-start | bytes 786440 | tf_op jit(solution)/shard_map/gather_queries/ppermute | solution.py:266
  22.2 14.7 %collective-permute-start.9 = (bf16[8,128,128]{2,1,0:T(8,128)(2,1)S(1)}, bf16[8,128,128]{2,1,0:T(8,128)(2,1)S(1)}, u32[]{:S(2)}, u32[]{:S(2)}) collective-permute-start(bf16[8,128,128]{2,1,0:T(8,128)(2,1)S(1)} %all-to-all-done.refs_0_), channel_id=1, source_target_pairs={{0,24},{8,16},{16,8},{24,0},{32,56},{40,48},{48,40},{56,32},{64,88... | collective-permute-start | bytes 786440 | tf_op jit(solution)/shard_map/gather_queries/ppermute | solution.py:266
  24.4 12.9 %collective-permute-start.10 = (bf16[8,128,128]{2,1,0:T(8,128)(2,1)S(1)}, bf16[8,128,128]{2,1,0:T(8,128)(2,1)S(1)}, u32[]{:S(2)}, u32[]{:S(2)}) collective-permute-start(bf16[8,128,128]{2,1,0:T(8,128)(2,1)S(1)} %all-to-all-done.refs_0_), channel_id=1, source_target_pairs={{0,8},{8,0},{16,24},{24,16},{32,40},{40,32},{48,56},{56,48},{64,72... | collective-permute-start | bytes 786440 | tf_op jit(solution)/shard_map/gather_queries/ppermute | solution.py:266
  27.0 1.2 %collective-permute-start.5 = (f32[32,128]{1,0:T(8,128)S(1)}, f32[32,128]{1,0:T(8,128)S(1)}, u32[]{:S(2)}, u32[]{:S(2)}) collective-permute-start(f32[32,128]{1,0:T(8,128)S(1)} %outer.1.refs_0_), channel_id=1, source_target_pairs={{0,1},{1,0},{2,3},{3,2},{4,5},{5,4},{6,7},{7,6},{8,9},{9,8},{10,11... | collective-permute-start | bytes 49160 | tf_op jit(solution)/shard_map/exchange_grad/ppermute | solution.py:259
  28.3 4.9 %collective-permute-start.6 = (f32[32,128]{1,0:T(8,128)S(1)}, f32[32,128]{1,0:T(8,128)S(1)}, u32[]{:S(2)}, u32[]{:S(2)}) collective-permute-start(f32[32,128]{1,0:T(8,128)S(1)} %sum_parts.2.refs_0_), channel_id=1, source_target_pairs={{0,6},{1,7},{2,4},{3,5},{4,2},{5,3},{6,0},{7,1},{8,14},{9,15},{10,... | collective-permute-start | bytes 49160 | tf_op jit(solution)/shard_map/exchange_grad/ppermute | solution.py:259
  33.2 3.7 %collective-permute-start.7 = (f32[32,128]{1,0:T(8,128)S(1)}, f32[32,128]{1,0:T(8,128)S(1)}, u32[]{:S(2)}, u32[]{:S(2)}) collective-permute-start(f32[32,128]{1,0:T(8,128)S(1)} %sum_parts.3.a_ref), channel_id=1, source_target_pairs={{0,2},{1,3},{2,0},{3,1},{4,6},{5,7},{6,4},{7,5},{8,10},{9,11},{10,... | collective-permute-start | bytes 49160 | tf_op jit(solution)/shard_map/exchange_grad/ppermute | solution.py:259

commit v4 on v3

--- a/solution.py
+++ b/solution.py
@@ -185,6 +185,23 @@
     )(*parts)
 
 
+def after_kernel(x_ref, _, out_ref):
+    out_ref[...] = x_ref[...]
+
+
+def after(x, other):
+    vmem = pl.BlockSpec(memory_space=pltpu.VMEM)
+    return pl.pallas_call(
+        after_kernel,
+        out_shape=jax.ShapeDtypeStruct(x.shape, x.dtype),
+        in_specs=[vmem, pl.BlockSpec(memory_space=pl.ANY)],
+        out_specs=vmem,
+        compiler_params=pltpu.CompilerParams(vmem_limit_bytes=SMALL_VMEM),
+        cost_estimate=NO_COST,
+        name="after",
+    )(x, other)
+
+
 def add_blocks(dots, squares, unit, q_ref):
     for z in range(q_ref.shape[0]):
         q = q_ref[z].astype(jnp.float32)
@@ -278,8 +295,8 @@
         partial = outer(core * chips + chip, row, token_mask.reshape(-1, BLOCK), parts)
     with jax.named_scope("exchange_grad"):
         pair = sum_parts([partial, swap(partial, 1)])
-        four = sum_parts([pair, swap(pair, 6)])
-        partials = [four, swap(four, 2)]
+        third = after(pair, gathered[1])
+        partials = [sum_parts([pair, swap(pair, 4), swap(pair, 6)]), swap(third, 2)]
     with jax.named_scope("score"):
         index = me * qlocal + jnp.arange(qlocal, dtype=jnp.int32)
         factor = jnp.where(index[None, :] == cand_ids[:, None], jnp.float32(0.0), jnp.float32(1.0 / rank))

time: 38.3 us -> 37.7 us (0.984)
  waiting for transfers between devices: 8.4 us -> 5.02 us
  starting transfers between devices: 20 us -> 22.6 us
    ppermute x8 -> x9, waiting for transfers between devices: 8.39 us -> 4.39 us  [swap(): return lax.ppermute(x, 'tensor', [(i, i ^ mask) for i in range(devices)])]
    ppermute x8 -> x9, starting transfers between devices: 7.86 us -> 10.4 us  [swap(): return lax.ppermute(x, 'tensor', [(i, i ^ mask) for i in range(devices)])]
    ppermute x3, waiting for transfers between devices: 0.01 us -> 0.62 us  [body(): lax.ppermute(column, 'dp', [(i, i ^ k) for i in range(dp)])]
  transfers between devices with their start and end apart: 12 -> 13, of which waited for: 5 -> 6; matrix products, arithmetic and copies ran while one was open for 0% -> 0% of each run, Pallas kernels for 17% -> 18%
where the time goes in v4:
time: 37.7 us; the launch traced here: 37.2 us
  starting transfers between devices  22.6 us (60%)
  Pallas kernels  7.32 us (19%)
  waiting for transfers between devices  5.02 us (13%)
  local copies, waits for them, and re-layouts  1.51 us (4%)
  between operations  0.75 us (2%)
    ppermute x9, starting transfers between devices, swap(): return lax.ppermute(x, 'tensor', [(i, i ^ mask) for i in range(devices)])  10.4 us
    all_to_all x1, starting transfers between devices, body(): lax.all_to_all(copies, 'dp', 0, 0, tiled=True, axis_index_groups=columns)  8.57 us
    pallas_call x1, Pallas kernels, project_theirs(): pl.pallas_call(functools.partial(theirs_kernel, n), out_shape=[jax.ShapeD...  4.5 us
    ppermute x9, waiting for transfers between devices, swap(): return lax.ppermute(x, 'tensor', [(i, i ^ mask) for i in range(devices)])  4.39 us
    ppermute x3, starting transfers between devices, body(): lax.ppermute(column, 'dp', [(i, i ^ k) for i in range(dp)])  3.62 us
    broadcast_in_dim x1, local copies, waits for them, and re-layouts, body(): copies = jnp.broadcast_to(queries[None], (layers, *queries.shape))  1.5 us
    pallas_call x1, Pallas kernels, project_mine(): pl.pallas_call(mine_kernel, out_shape=[jax.ShapeDtypeStruct((BLOCK, w.sha...  1.36 us
  transfers between devices with their start and end apart: 13, of which 6 were waited for; matrix products, arithmetic and copies ran while one was open for 0% of the time, Pallas kernels for 18%

profile of v4, /device:TPU:56, one launch (start us, length us, event | category | flops | bytes accessed | tf_op | source)
XLA Modules:
  0.0 37.2 jit_solution(4200171485242138573)
XLA Ops:
  0.0 1.5 %broadcast_in_dim.34 = bf16[8,128,128]{2,1,0:T(8,128)(2,1)} broadcast(bf16[128,128]{1,0:T(8,128)(2,1)} %param.13), dimensions={1,2} | broadcast | bytes 294912 | tf_op jit(solution)/shard_map/gather_queries/broadcast_in_dim | solution.py:281
  1.5 8.6 %all-to-all-start = ((bf16[8,128,128]{2,1,0:T(8,128)(2,1)}), bf16[8,128,128]{2,1,0:T(8,128)(2,1)S(1)}, u32[]{:S(2)}, u32[]{:S(2)}) async-start(bf16[8,128,128]{2,1,0:T(8,128)(2,1)} %broadcast_in_dim.34), calls=%async_computation | async-start | bytes 524288 | tf_op jit(solution)/shard_map/gather_queries/all_to_all | solution.py:282
  10.1 4.5 %project_theirs.1 = (f32[512,128]{1,0:T(8,128)S(1)}, f32[512,128]{1,0:T(8,128)S(1)}, bf16[1024,1792]{1,0:T(8,128)(2,1)S(1)}, bf16[1024,512]{1,0:T(8,128)(2,1)S(1)}, bf16[128,2304]{1,0:T(8,128)(2,1)S(1)}) custom-call(s32[1]{0:T(128)} %bitcast.3.core_ref, s32[1]{0:T(128)} %bitcast.4.chip_ref, bf16[2048,1792]{1,0:T(8,128)(2,1)} %hidden_ref.1, ...), custom_call_target="tpu_custom_call" | custom-call | tf_op jit(solution)/shard_map/project/project_theirs/pallas_call | solution.py:75
  14.6 0.0 copy-start
  14.6 0.1 collective-permute-start
  14.7 0.5 %collective-permute-start.1 = (f32[512,128]{1,0:T(8,128)S(1)}, f32[512,128]{1,0:T(8,128)S(1)}, u32[]{:S(2)}, u32[]{:S(2)}) collective-permute-start(f32[512,128]{1,0:T(8,128)S(1)} %get-tuple-element.29), channel_id=1, source_target_pairs={{0,1},{1,0},{2,3},{3,2},{4,5},{5,4},{6,7},{7,6},{8,9},{9,8},{10,11... | collective-permute-start | bytes 786440 | tf_op jit(solution)/shard_map/project/ppermute | solution.py:276
  15.2 1.4 %project_mine.1 = (f32[256,128]{1,0:T(8,128)S(1)}, f32[256,128]{1,0:T(8,128)S(1)}, f32[256,128]{1,0:T(8,128)S(1)}, f32[256,128]{1,0:T(8,128)S(1)}) custom-call(bf16[1024,1792]{1,0:T(8,128)(2,1)S(1)} %get-tuple-element.21.hidden_ref, bf16[1024,512]{1,0:T(8,128)(2,1)S(1)} %get-tuple-element.22.grad_ref, bf16[128,2304]{1,0:T(8,128)(2,1)S(1)} %get-tuple-element.23.w_ref), custom_call_target="tpu_custom_call" | custom-call | tf_op jit(solution)/shard_map/project/project_mine/pallas_call | solution.py:108
  16.6 0.0 collective-permute-done.refs_4_
  16.6 0.0 collective-permute-done.1.refs_5_
  16.6 0.1 pair_sum.1
  16.6 3.1 %collective-permute-start.2 = (f32[256,128]{1,0:T(8,128)S(1)}, f32[256,128]{1,0:T(8,128)S(1)}, u32[]{:S(2)}, u32[]{:S(2)}) collective-permute-start(f32[256,128]{1,0:T(8,128)S(1)} %get-tuple-element.31), channel_id=1, source_target_pairs={{0,4},{1,5},{2,6},{3,7},{4,0},{5,1},{6,2},{7,3},{8,12},{9,13},{10,... | collective-permute-start | bytes 393224 | tf_op jit(solution)/shard_map/exchange_tokens/ppermute | solution.py:276
  19.8 1.1 %collective-permute-start.3 = (f32[256,128]{1,0:T(8,128)S(1)}, f32[256,128]{1,0:T(8,128)S(1)}, u32[]{:S(2)}, u32[]{:S(2)}) collective-permute-start(f32[256,128]{1,0:T(8,128)S(1)} %get-tuple-element.32), channel_id=1, source_target_pairs={{0,6},{1,7},{2,4},{3,5},{4,2},{5,3},{6,0},{7,1},{8,14},{9,15},{10,... | collective-permute-start | bytes 393224 | tf_op jit(solution)/shard_map/exchange_tokens/ppermute | solution.py:276
  20.9 0.0 collective-permute-start.4
  20.9 0.0 all-to-all-done.refs_0_
  20.9 1.3 %collective-permute-start.8 = (bf16[8,128,128]{2,1,0:T(8,128)(2,1)S(1)}, bf16[8,128,128]{2,1,0:T(8,128)(2,1)S(1)}, u32[]{:S(2)}, u32[]{:S(2)}) collective-permute-start(bf16[8,128,128]{2,1,0:T(8,128)(2,1)S(1)} %all-to-all-done.refs_0_), channel_id=1, source_target_pairs={{0,16},{8,24},{16,0},{24,8},{32,48},{40,56},{48,32},{56,40},{64,80... | collective-permute-start | bytes 786440 | tf_op jit(solution)/shard_map/gather_queries/ppermute | solution.py:283
  22.3 2.2 %collective-permute-start.10 = (bf16[8,128,128]{2,1,0:T(8,128)(2,1)S(1)}, bf16[8,128,128]{2,1,0:T(8,128)(2,1)S(1)}, u32[]{:S(2)}, u32[]{:S(2)}) collective-permute-start(bf16[8,128,128]{2,1,0:T(8,128)(2,1)S(1)} %all-to-all-done.refs_0_), channel_id=1, source_target_pairs={{0,24},{8,16},{16,8},{24,0},{32,56},{40,48},{48,40},{56,32},{64,88... | collective-permute-start | bytes 786440 | tf_op jit(solution)/shard_map/gather_queries/ppermute | solution.py:283
  24.4 0.0 collective-permute-done.2.refs_1_
  24.4 0.1 collective-permute-start.11
  24.6 2.0 %collective-permute-done.3.refs_2_ = f32[256,128]{1,0:T(8,128)S(1)} collective-permute-done((f32[256,128]{1,0:T(8,128)S(1)}, f32[256,128]{1,0:T(8,128)S(1)}, u32[]{:S(2)}, u32[]{:S(2)}) %collective-permute-start.3) | collective-permute-done | bytes 131104 | tf_op jit(solution)/shard_map/exchange_tokens/ppermute | solution.py:276
  26.6 0.1 collective-permute-done.4.refs_3_
  26.7 0.4 outer.1.refs_0_
  27.0 0.1 collective-permute-start.5
  27.8 0.5 %collective-permute-done.5.refs_1_ = f32[32,128]{1,0:T(8,128)S(1)} collective-permute-done((f32[32,128]{1,0:T(8,128)S(1)}, f32[32,128]{1,0:T(8,128)S(1)}, u32[]{:S(2)}, u32[]{:S(2)}) %collective-permute-start.5) | collective-permute-done | bytes 16416 | tf_op jit(solution)/shard_map/exchange_grad/ppermute | solution.py:276
  28.3 2.1 %collective-permute-start.6 = (f32[32,128]{1,0:T(8,128)S(1)}, f32[32,128]{1,0:T(8,128)S(1)}, u32[]{:S(2)}, u32[]{:S(2)}) collective-permute-start(f32[32,128]{1,0:T(8,128)S(1)} %sum_parts.2.refs_0_.x_ref), channel_id=1, source_target_pairs={{0,4},{1,5},{2,6},{3,7},{4,0},{5,1},{6,2},{7,3},{8,12},{9,13},{10,... | collective-permute-start | bytes 49160 | tf_op jit(solution)/shard_map/exchange_grad/ppermute | solution.py:276
  30.4 2.1 %collective-permute-start.7 = (f32[32,128]{1,0:T(8,128)S(1)}, f32[32,128]{1,0:T(8,128)S(1)}, u32[]{:S(2)}, u32[]{:S(2)}) collective-permute-start(f32[32,128]{1,0:T(8,128)S(1)} %sum_parts.2.refs_0_.x_ref), channel_id=1, source_target_pairs={{0,6},{1,7},{2,4},{3,5},{4,2},{5,3},{6,0},{7,1},{8,14},{9,15},{10,... | collective-permute-start | bytes 49160 | tf_op jit(solution)/shard_map/exchange_grad/ppermute | solution.py:276
  32.4 0.0 collective-permute-done.8._.refs_1_
  32.4 1.4 %collective-permute-start.9 = (f32[32,128]{1,0:T(8,128)S(1)}, f32[32,128]{1,0:T(8,128)S(1)}, u32[]{:S(2)}, u32[]{:S(2)}) collective-permute-start(f32[32,128]{1,0:T(8,128)S(1)} %after.1), channel_id=1, source_target_pairs={{0,2},{1,3},{2,0},{3,1},{4,6},{5,7},{6,4},{7,5},{8,10},{9,11},{10,... | collective-permute-start | bytes 49160 | tf_op jit(solution)/shard_map/exchange_grad/ppermute | solution.py:276
  33.8 1.5 %collective-permute-done.7.refs_2_ = f32[32,128]{1,0:T(8,128)S(1)} collective-permute-done((f32[32,128]{1,0:T(8,128)S(1)}, f32[32,128]{1,0:T(8,128)S(1)}, u32[]{:S(2)}, u32[]{:S(2)}) %collective-permute-start.7) | collective-permute-done | bytes 16416 | tf_op jit(solution)/shard_map/exchange_grad/ppermute | solution.py:276
  35.3 0.6 %collective-permute-done.10.refs_2_ = bf16[8,128,128]{2,1,0:T(8,128)(2,1)S(1)} collective-permute-done((bf16[8,128,128]{2,1,0:T(8,128)(2,1)S(1)}, bf16[8,128,128]{2,1,0:T(8,128)(2,1)S(1)}, u32[]{:S(2)}, u32[]{:S(2)}) %collective-permute-start.10) | collective-permute-done | bytes 262176 | tf_op jit(solution)/shard_map/gather_queries/ppermute | solution.py:283
  35.9 0.3 collective-permute-done.9.b_ref
  36.2 0.3 score_start.1
  36.5 0.7 %score.1 = f32[1,128]{1,0:T(1,128)} custom-call(f32[1,128]{1,0:T(1,128)S(1)} %compare_select_fusion.factor_ref, f32[8,128]{1,0:T(8,128)S(1)} %get-tuple-element.34.unit_ref, f32[128,128]{1,0:T(8,128)S(1)} %get-tuple-element.35.dots_ref, f32[128,128]{1,0:T(8,128)S(1)} %get-tuple-element.36.squares_ref, bf16[8,128,128]{2,1,0:T(8,128)(2,1)S(1)} %collective-permute-done.11.q_ref), custom_call_target="tpu_custom_call" | custom-call | tf_op jit(solution)/shard_map/score/score/pallas_call | solution.py:251
  (8 shorter events, 0.0 us)
Async XLA Ops:
  1.5 19.4 %all-to-all-start = ((bf16[8,128,128]{2,1,0:T(8,128)(2,1)}), bf16[8,128,128]{2,1,0:T(8,128)(2,1)S(1)}, u32[]{:S(2)}, u32[]{:S(2)}) async-start(bf16[8,128,128]{2,1,0:T(8,128)(2,1)} %broadcast_in_dim.34), calls=%async_computation | async-start | bytes 524288 | tf_op jit(solution)/shard_map/gather_queries/all_to_all | solution.py:282
  14.6 6.3 %copy-start = (s32[2048]{0:T(1024)S(1)}, s32[2048]{0:T(1024)}, u32[]{:S(2)}) copy-start(s32[2048]{0:T(1024)} %param.11) | copy-start | bytes 24580
  14.6 2.0 %collective-permute-start = (f32[512,128]{1,0:T(8,128)S(1)}, f32[512,128]{1,0:T(8,128)S(1)}, u32[]{:S(2)}, u32[]{:S(2)}) collective-permute-start(f32[512,128]{1,0:T(8,128)S(1)} %get-tuple-element.28), channel_id=1, source_target_pairs={{0,1},{1,0},{2,3},{3,2},{4,5},{5,4},{6,7},{7,6},{8,9},{9,8},{10,11... | collective-permute-start | bytes 786440 | tf_op jit(solution)/shard_map/project/ppermute | solution.py:276
  14.7 1.9 %collective-permute-start.1 = (f32[512,128]{1,0:T(8,128)S(1)}, f32[512,128]{1,0:T(8,128)S(1)}, u32[]{:S(2)}, u32[]{:S(2)}) collective-permute-start(f32[512,128]{1,0:T(8,128)S(1)} %get-tuple-element.29), channel_id=1, source_target_pairs={{0,1},{1,0},{2,3},{3,2},{4,5},{5,4},{6,7},{7,6},{8,9},{9,8},{10,11... | collective-permute-start | bytes 786440 | tf_op jit(solution)/shard_map/project/ppermute | solution.py:276
  16.6 7.8 %collective-permute-start.2 = (f32[256,128]{1,0:T(8,128)S(1)}, f32[256,128]{1,0:T(8,128)S(1)}, u32[]{:S(2)}, u32[]{:S(2)}) collective-permute-start(f32[256,128]{1,0:T(8,128)S(1)} %get-tuple-element.31), channel_id=1, source_target_pairs={{0,4},{1,5},{2,6},{3,7},{4,0},{5,1},{6,2},{7,3},{8,12},{9,13},{10,... | collective-permute-start | bytes 393224 | tf_op jit(solution)/shard_map/exchange_tokens/ppermute | solution.py:276
  19.8 6.8 %collective-permute-start.3 = (f32[256,128]{1,0:T(8,128)S(1)}, f32[256,128]{1,0:T(8,128)S(1)}, u32[]{:S(2)}, u32[]{:S(2)}) collective-permute-start(f32[256,128]{1,0:T(8,128)S(1)} %get-tuple-element.32), channel_id=1, source_target_pairs={{0,6},{1,7},{2,4},{3,5},{4,2},{5,3},{6,0},{7,1},{8,14},{9,15},{10,... | collective-permute-start | bytes 393224 | tf_op jit(solution)/shard_map/exchange_tokens/ppermute | solution.py:276
  20.9 5.8 %collective-permute-start.4 = (f32[256,128]{1,0:T(8,128)S(1)}, f32[256,128]{1,0:T(8,128)S(1)}, u32[]{:S(2)}, u32[]{:S(2)}) collective-permute-start(f32[256,128]{1,0:T(8,128)S(1)} %get-tuple-element.33), channel_id=1, source_target_pairs={{0,2},{1,3},{2,0},{3,1},{4,6},{5,7},{6,4},{7,5},{8,10},{9,11},{10,... | collective-permute-start | bytes 393224 | tf_op jit(solution)/shard_map/exchange_tokens/ppermute | solution.py:276
  20.9 11.5 %collective-permute-start.8 = (bf16[8,128,128]{2,1,0:T(8,128)(2,1)S(1)}, bf16[8,128,128]{2,1,0:T(8,128)(2,1)S(1)}, u32[]{:S(2)}, u32[]{:S(2)}) collective-permute-start(bf16[8,128,128]{2,1,0:T(8,128)(2,1)S(1)} %all-to-all-done.refs_0_), channel_id=1, source_target_pairs={{0,16},{8,24},{16,0},{24,8},{32,48},{40,56},{48,32},{56,40},{64,80... | collective-permute-start | bytes 786440 | tf_op jit(solution)/shard_map/gather_queries/ppermute | solution.py:283
  22.3 13.7 %collective-permute-start.10 = (bf16[8,128,128]{2,1,0:T(8,128)(2,1)S(1)}, bf16[8,128,128]{2,1,0:T(8,128)(2,1)S(1)}, u32[]{:S(2)}, u32[]{:S(2)}) collective-permute-start(bf16[8,128,128]{2,1,0:T(8,128)(2,1)S(1)} %all-to-all-done.refs_0_), channel_id=1, source_target_pairs={{0,24},{8,16},{16,8},{24,0},{32,56},{40,48},{48,40},{56,32},{64,88... | collective-permute-start | bytes 786440 | tf_op jit(solution)/shard_map/gather_queries/ppermute | solution.py:283
  24.4 12.1 %collective-permute-start.11 = (bf16[8,128,128]{2,1,0:T(8,128)(2,1)S(1)}, bf16[8,128,128]{2,1,0:T(8,128)(2,1)S(1)}, u32[]{:S(2)}, u32[]{:S(2)}) collective-permute-start(bf16[8,128,128]{2,1,0:T(8,128)(2,1)S(1)} %all-to-all-done.refs_0_), channel_id=1, source_target_pairs={{0,8},{8,0},{16,24},{24,16},{32,40},{40,32},{48,56},{56,48},{64,72... | collective-permute-start | bytes 786440 | tf_op jit(solution)/shard_map/gather_queries/ppermute | solution.py:283
  27.0 1.2 %collective-permute-start.5 = (f32[32,128]{1,0:T(8,128)S(1)}, f32[32,128]{1,0:T(8,128)S(1)}, u32[]{:S(2)}, u32[]{:S(2)}) collective-permute-start(f32[32,128]{1,0:T(8,128)S(1)} %outer.1.refs_0_), channel_id=1, source_target_pairs={{0,1},{1,0},{2,3},{3,2},{4,5},{5,4},{6,7},{7,6},{8,9},{9,8},{10,11... | collective-permute-start | bytes 49160 | tf_op jit(solution)/shard_map/exchange_grad/ppermute | solution.py:276
  28.3 5.5 %collective-permute-start.6 = (f32[32,128]{1,0:T(8,128)S(1)}, f32[32,128]{1,0:T(8,128)S(1)}, u32[]{:S(2)}, u32[]{:S(2)}) collective-permute-start(f32[32,128]{1,0:T(8,128)S(1)} %sum_parts.2.refs_0_.x_ref), channel_id=1, source_target_pairs={{0,4},{1,5},{2,6},{3,7},{4,0},{5,1},{6,2},{7,3},{8,12},{9,13},{10,... | collective-permute-start | bytes 49160 | tf_op jit(solution)/shard_map/exchange_grad/ppermute | solution.py:276
  30.4 4.9 %collective-permute-start.7 = (f32[32,128]{1,0:T(8,128)S(1)}, f32[32,128]{1,0:T(8,128)S(1)}, u32[]{:S(2)}, u32[]{:S(2)}) collective-permute-start(f32[32,128]{1,0:T(8,128)S(1)} %sum_parts.2.refs_0_.x_ref), channel_id=1, source_target_pairs={{0,6},{1,7},{2,4},{3,5},{4,2},{5,3},{6,0},{7,1},{8,14},{9,15},{10,... | collective-permute-start | bytes 49160 | tf_op jit(solution)/shard_map/exchange_grad/ppermute | solution.py:276
  32.4 3.7 %collective-permute-start.9 = (f32[32,128]{1,0:T(8,128)S(1)}, f32[32,128]{1,0:T(8,128)S(1)}, u32[]{:S(2)}, u32[]{:S(2)}) collective-permute-start(f32[32,128]{1,0:T(8,128)S(1)} %after.1), channel_id=1, source_target_pairs={{0,2},{1,3},{2,0},{3,1},{4,6},{5,7},{6,4},{7,5},{8,10},{9,11},{10,... | collective-permute-start | bytes 49160 | tf_op jit(solution)/shard_map/exchange_grad/ppermute | solution.py:276

commit v5 on v4

--- a/solution.py
+++ b/solution.py
@@ -210,9 +210,9 @@
     return dots, squares
 
 
-def start_kernel(a_ref, b_ref, *refs):
-    q_refs, (last_ref, dots_ref, squares_ref) = refs[:-3], refs[-3:]
-    grad = a_ref[...] + b_ref[...]
+def start_kernel(n, *refs):
+    parts, q_refs, (last_ref, dots_ref, squares_ref) = refs[:n], refs[n:-3], refs[-3:]
+    grad = functools.reduce(lambda a, b: a + b, [r[...] for r in parts])
     mean = jnp.sum(grad * grad, keepdims=True) / grad.size
     unit = (grad / jnp.sqrt(mean + 1e-06)).astype(jnp.bfloat16).astype(jnp.float32)
     layers = q_refs[0].shape[0]
@@ -229,7 +229,7 @@
     layers, qlocal, lanes = q[0].shape
     sums = jax.ShapeDtypeStruct((qlocal, lanes), jnp.float32)
     return pl.pallas_call(
-        start_kernel,
+        functools.partial(start_kernel, len(parts)),
         out_shape=[jax.ShapeDtypeStruct((layers, lanes), jnp.float32), sums, sums],
         in_specs=[vmem] * (len(parts) + len(q)),
         out_specs=[vmem] * 3,
@@ -296,7 +296,7 @@
     with jax.named_scope("exchange_grad"):
         pair = sum_parts([partial, swap(partial, 1)])
         third = after(pair, gathered[1])
-        partials = [sum_parts([pair, swap(pair, 4), swap(pair, 6)]), swap(third, 2)]
+        partials = [pair, swap(pair, 6), swap(pair, 4), swap(third, 2)]
     with jax.named_scope("score"):
         index = me * qlocal + jnp.arange(qlocal, dtype=jnp.int32)
         factor = jnp.where(index[None, :] == cand_ids[:, None], jnp.float32(0.0), jnp.float32(1.0 / rank))

time: 37.7 us -> 37.7 us (level)
    ppermute x9, waiting for transfers between devices: 4.39 us -> 5.04 us  [swap(): return lax.ppermute(x, 'tensor', [(i, i ^ mask) for i in range(devices)])]
    ppermute x3, waiting for transfers between devices: 0.62 us -> 0.01 us  [body(): lax.ppermute(column, 'dp', [(i, i ^ k) for i in range(dp)])]
  transfers between devices with their start and end apart: 13 -> 13, of which waited for: 6 -> 4; matrix products, arithmetic and copies ran while one was open for 0% -> 0% of each run, Pallas kernels for 18% -> 18%
where the time goes in v5:
time: 37.7 us; the launch traced here: 37.3 us
  starting transfers between devices  22.6 us (60%)
  Pallas kernels  7.32 us (19%)
  waiting for transfers between devices  5.05 us (13%)
  local copies, waits for them, and re-layouts  1.51 us (4%)
  between operations  0.75 us (2%)
    ppermute x9, starting transfers between devices, swap(): return lax.ppermute(x, 'tensor', [(i, i ^ mask) for i in range(devices)])  10.4 us
    all_to_all x1, starting transfers between devices, body(): lax.all_to_all(copies, 'dp', 0, 0, tiled=True, axis_index_groups=columns)  8.57 us
    ppermute x9, waiting for transfers between devices, swap(): return lax.ppermute(x, 'tensor', [(i, i ^ mask) for i in range(devices)])  5.04 us
    pallas_call x1, Pallas kernels, project_theirs(): pl.pallas_call(functools.partial(theirs_kernel, n), out_shape=[jax.ShapeD...  4.5 us
    ppermute x3, starting transfers between devices, body(): lax.ppermute(column, 'dp', [(i, i ^ k) for i in range(dp)])  3.62 us
    broadcast_in_dim x1, local copies, waits for them, and re-layouts, body(): copies = jnp.broadcast_to(queries[None], (layers, *queries.shape))  1.5 us
    pallas_call x1, Pallas kernels, project_mine(): pl.pallas_call(mine_kernel, out_shape=[jax.ShapeDtypeStruct((BLOCK, w.sha...  1.36 us
  transfers between devices with their start and end apart: 13, of which 4 were waited for; matrix products, arithmetic and copies ran while one was open for 0% of the time, Pallas kernels for 18%

profile of v5, /device:TPU:56, one launch (start us, length us, event | category | flops | bytes accessed | tf_op | source)
XLA Modules:
  0.0 37.3 jit_solution(8135405931262278498)
XLA Ops:
  0.0 1.5 %broadcast_in_dim.34 = bf16[8,128,128]{2,1,0:T(8,128)(2,1)} broadcast(bf16[128,128]{1,0:T(8,128)(2,1)} %param.13), dimensions={1,2} | broadcast | bytes 294912 | tf_op jit(solution)/shard_map/gather_queries/broadcast_in_dim | solution.py:281
  1.5 8.6 %all-to-all-start = ((bf16[8,128,128]{2,1,0:T(8,128)(2,1)}), bf16[8,128,128]{2,1,0:T(8,128)(2,1)S(1)}, u32[]{:S(2)}, u32[]{:S(2)}) async-start(bf16[8,128,128]{2,1,0:T(8,128)(2,1)} %broadcast_in_dim.34), calls=%async_computation | async-start | bytes 524288 | tf_op jit(solution)/shard_map/gather_queries/all_to_all | solution.py:282
  10.1 4.5 %project_theirs.1 = (f32[512,128]{1,0:T(8,128)S(1)}, f32[512,128]{1,0:T(8,128)S(1)}, bf16[1024,1792]{1,0:T(8,128)(2,1)S(1)}, bf16[1024,512]{1,0:T(8,128)(2,1)S(1)}, bf16[128,2304]{1,0:T(8,128)(2,1)S(1)}) custom-call(s32[1]{0:T(128)} %bitcast.3.core_ref, s32[1]{0:T(128)} %bitcast.4.chip_ref, bf16[2048,1792]{1,0:T(8,128)(2,1)} %hidden_ref.1, ...), custom_call_target="tpu_custom_call" | custom-call | tf_op jit(solution)/shard_map/project/project_theirs/pallas_call | solution.py:75
  14.6 0.0 copy-start
  14.6 0.1 collective-permute-start
  14.7 0.5 %collective-permute-start.1 = (f32[512,128]{1,0:T(8,128)S(1)}, f32[512,128]{1,0:T(8,128)S(1)}, u32[]{:S(2)}, u32[]{:S(2)}) collective-permute-start(f32[512,128]{1,0:T(8,128)S(1)} %get-tuple-element.29), channel_id=1, source_target_pairs={{0,1},{1,0},{2,3},{3,2},{4,5},{5,4},{6,7},{7,6},{8,9},{9,8},{10,11... | collective-permute-start | bytes 786440 | tf_op jit(solution)/shard_map/project/ppermute | solution.py:276
  15.2 1.4 %project_mine.1 = (f32[256,128]{1,0:T(8,128)S(1)}, f32[256,128]{1,0:T(8,128)S(1)}, f32[256,128]{1,0:T(8,128)S(1)}, f32[256,128]{1,0:T(8,128)S(1)}) custom-call(bf16[1024,1792]{1,0:T(8,128)(2,1)S(1)} %get-tuple-element.21.hidden_ref, bf16[1024,512]{1,0:T(8,128)(2,1)S(1)} %get-tuple-element.22.grad_ref, bf16[128,2304]{1,0:T(8,128)(2,1)S(1)} %get-tuple-element.23.w_ref), custom_call_target="tpu_custom_call" | custom-call | tf_op jit(solution)/shard_map/project/project_mine/pallas_call | solution.py:108
  16.6 0.0 collective-permute-done.refs_4_
  16.6 0.0 collective-permute-done.1.refs_5_
  16.6 0.1 pair_sum.1
  16.6 3.1 %collective-permute-start.2 = (f32[256,128]{1,0:T(8,128)S(1)}, f32[256,128]{1,0:T(8,128)S(1)}, u32[]{:S(2)}, u32[]{:S(2)}) collective-permute-start(f32[256,128]{1,0:T(8,128)S(1)} %get-tuple-element.31), channel_id=1, source_target_pairs={{0,4},{1,5},{2,6},{3,7},{4,0},{5,1},{6,2},{7,3},{8,12},{9,13},{10,... | collective-permute-start | bytes 393224 | tf_op jit(solution)/shard_map/exchange_tokens/ppermute | solution.py:276
  19.8 1.1 %collective-permute-start.3 = (f32[256,128]{1,0:T(8,128)S(1)}, f32[256,128]{1,0:T(8,128)S(1)}, u32[]{:S(2)}, u32[]{:S(2)}) collective-permute-start(f32[256,128]{1,0:T(8,128)S(1)} %get-tuple-element.32), channel_id=1, source_target_pairs={{0,6},{1,7},{2,4},{3,5},{4,2},{5,3},{6,0},{7,1},{8,14},{9,15},{10,... | collective-permute-start | bytes 393224 | tf_op jit(solution)/shard_map/exchange_tokens/ppermute | solution.py:276
  20.9 0.0 collective-permute-start.4
  20.9 0.0 all-to-all-done.refs_4_
  20.9 1.3 %collective-permute-start.8 = (bf16[8,128,128]{2,1,0:T(8,128)(2,1)S(1)}, bf16[8,128,128]{2,1,0:T(8,128)(2,1)S(1)}, u32[]{:S(2)}, u32[]{:S(2)}) collective-permute-start(bf16[8,128,128]{2,1,0:T(8,128)(2,1)S(1)} %all-to-all-done.refs_4_), channel_id=1, source_target_pairs={{0,16},{8,24},{16,0},{24,8},{32,48},{40,56},{48,32},{56,40},{64,80... | collective-permute-start | bytes 786440 | tf_op jit(solution)/shard_map/gather_queries/ppermute | solution.py:283
  22.3 2.2 %collective-permute-start.10 = (bf16[8,128,128]{2,1,0:T(8,128)(2,1)S(1)}, bf16[8,128,128]{2,1,0:T(8,128)(2,1)S(1)}, u32[]{:S(2)}, u32[]{:S(2)}) collective-permute-start(bf16[8,128,128]{2,1,0:T(8,128)(2,1)S(1)} %all-to-all-done.refs_4_), channel_id=1, source_target_pairs={{0,24},{8,16},{16,8},{24,0},{32,56},{40,48},{48,40},{56,32},{64,88... | collective-permute-start | bytes 786440 | tf_op jit(solution)/shard_map/gather_queries/ppermute | solution.py:283
  24.4 0.0 collective-permute-done.2.refs_1_
  24.4 0.1 collective-permute-start.11
  24.6 2.0 %collective-permute-done.3.refs_2_ = f32[256,128]{1,0:T(8,128)S(1)} collective-permute-done((f32[256,128]{1,0:T(8,128)S(1)}, f32[256,128]{1,0:T(8,128)S(1)}, u32[]{:S(2)}, u32[]{:S(2)}) %collective-permute-start.3) | collective-permute-done | bytes 131104 | tf_op jit(solution)/shard_map/exchange_tokens/ppermute | solution.py:276
  26.6 0.1 collective-permute-done.4.refs_3_
  26.7 0.4 outer.1.refs_0_
  27.0 0.1 collective-permute-start.5
  27.8 0.5 %collective-permute-done.5.refs_1_ = f32[32,128]{1,0:T(8,128)S(1)} collective-permute-done((f32[32,128]{1,0:T(8,128)S(1)}, f32[32,128]{1,0:T(8,128)S(1)}, u32[]{:S(2)}, u32[]{:S(2)}) %collective-permute-start.5) | collective-permute-done | bytes 16416 | tf_op jit(solution)/shard_map/exchange_grad/ppermute | solution.py:276
  28.3 2.7 %collective-permute-start.6 = (f32[32,128]{1,0:T(8,128)S(1)}, f32[32,128]{1,0:T(8,128)S(1)}, u32[]{:S(2)}, u32[]{:S(2)}) collective-permute-start(f32[32,128]{1,0:T(8,128)S(1)} %sum_parts.1.x_ref.refs_0_), channel_id=1, source_target_pairs={{0,6},{1,7},{2,4},{3,5},{4,2},{5,3},{6,0},{7,1},{8,14},{9,15},{10,... | collective-permute-start | bytes 49160 | tf_op jit(solution)/shard_map/exchange_grad/ppermute | solution.py:276
  31.0 0.9 %collective-permute-start.7 = (f32[32,128]{1,0:T(8,128)S(1)}, f32[32,128]{1,0:T(8,128)S(1)}, u32[]{:S(2)}, u32[]{:S(2)}) collective-permute-start(f32[32,128]{1,0:T(8,128)S(1)} %sum_parts.1.x_ref.refs_0_), channel_id=1, source_target_pairs={{0,4},{1,5},{2,6},{3,7},{4,0},{5,1},{6,2},{7,3},{8,12},{9,13},{10,... | collective-permute-start | bytes 49160 | tf_op jit(solution)/shard_map/exchange_grad/ppermute | solution.py:276
  31.8 2.0 %collective-permute-start.9 = (f32[32,128]{1,0:T(8,128)S(1)}, f32[32,128]{1,0:T(8,128)S(1)}, u32[]{:S(2)}, u32[]{:S(2)}) collective-permute-start(f32[32,128]{1,0:T(8,128)S(1)} %after.1), channel_id=1, source_target_pairs={{0,2},{1,3},{2,0},{3,1},{4,6},{5,7},{6,4},{7,5},{8,10},{9,11},{10,... | collective-permute-start | bytes 49160 | tf_op jit(solution)/shard_map/exchange_grad/ppermute | solution.py:276
  33.8 2.4 %collective-permute-done.7.refs_2_ = f32[32,128]{1,0:T(8,128)S(1)} collective-permute-done((f32[32,128]{1,0:T(8,128)S(1)}, f32[32,128]{1,0:T(8,128)S(1)}, u32[]{:S(2)}, u32[]{:S(2)}) %collective-permute-start.7) | collective-permute-done | bytes 16416 | tf_op jit(solution)/shard_map/exchange_grad/ppermute | solution.py:276
  36.2 0.0 collective-permute-done.10.refs_6_
  36.2 0.0 collective-permute-done.9.refs_3_
  36.2 0.3 score_start.1
  36.6 0.0 collective-permute-done.11.q_ref
  36.6 0.7 %score.1 = f32[1,128]{1,0:T(1,128)} custom-call(f32[1,128]{1,0:T(1,128)S(1)} %compare_select_fusion.factor_ref, f32[8,128]{1,0:T(8,128)S(1)} %get-tuple-element.34.unit_ref, f32[128,128]{1,0:T(8,128)S(1)} %get-tuple-element.35.dots_ref, f32[128,128]{1,0:T(8,128)S(1)} %get-tuple-element.36.squares_ref, bf16[8,128,128]{2,1,0:T(8,128)(2,1)S(1)} %collective-permute-done.11.q_ref), custom_call_target="tpu_custom_call" | custom-call | tf_op jit(solution)/shard_map/score/score/pallas_call | solution.py:251
  (7 shorter events, 0.0 us)
Async XLA Ops:
  1.5 19.4 %all-to-all-start = ((bf16[8,128,128]{2,1,0:T(8,128)(2,1)}), bf16[8,128,128]{2,1,0:T(8,128)(2,1)S(1)}, u32[]{:S(2)}, u32[]{:S(2)}) async-start(bf16[8,128,128]{2,1,0:T(8,128)(2,1)} %broadcast_in_dim.34), calls=%async_computation | async-start | bytes 524288 | tf_op jit(solution)/shard_map/gather_queries/all_to_all | solution.py:282
  14.6 6.3 %copy-start = (s32[2048]{0:T(1024)S(1)}, s32[2048]{0:T(1024)}, u32[]{:S(2)}) copy-start(s32[2048]{0:T(1024)} %param.11) | copy-start | bytes 24580
  14.6 2.0 %collective-permute-start = (f32[512,128]{1,0:T(8,128)S(1)}, f32[512,128]{1,0:T(8,128)S(1)}, u32[]{:S(2)}, u32[]{:S(2)}) collective-permute-start(f32[512,128]{1,0:T(8,128)S(1)} %get-tuple-element.28), channel_id=1, source_target_pairs={{0,1},{1,0},{2,3},{3,2},{4,5},{5,4},{6,7},{7,6},{8,9},{9,8},{10,11... | collective-permute-start | bytes 786440 | tf_op jit(solution)/shard_map/project/ppermute | solution.py:276
  14.7 1.9 %collective-permute-start.1 = (f32[512,128]{1,0:T(8,128)S(1)}, f32[512,128]{1,0:T(8,128)S(1)}, u32[]{:S(2)}, u32[]{:S(2)}) collective-permute-start(f32[512,128]{1,0:T(8,128)S(1)} %get-tuple-element.29), channel_id=1, source_target_pairs={{0,1},{1,0},{2,3},{3,2},{4,5},{5,4},{6,7},{7,6},{8,9},{9,8},{10,11... | collective-permute-start | bytes 786440 | tf_op jit(solution)/shard_map/project/ppermute | solution.py:276
  16.6 7.8 %collective-permute-start.2 = (f32[256,128]{1,0:T(8,128)S(1)}, f32[256,128]{1,0:T(8,128)S(1)}, u32[]{:S(2)}, u32[]{:S(2)}) collective-permute-start(f32[256,128]{1,0:T(8,128)S(1)} %get-tuple-element.31), channel_id=1, source_target_pairs={{0,4},{1,5},{2,6},{3,7},{4,0},{5,1},{6,2},{7,3},{8,12},{9,13},{10,... | collective-permute-start | bytes 393224 | tf_op jit(solution)/shard_map/exchange_tokens/ppermute | solution.py:276
  19.8 6.8 %collective-permute-start.3 = (f32[256,128]{1,0:T(8,128)S(1)}, f32[256,128]{1,0:T(8,128)S(1)}, u32[]{:S(2)}, u32[]{:S(2)}) collective-permute-start(f32[256,128]{1,0:T(8,128)S(1)} %get-tuple-element.32), channel_id=1, source_target_pairs={{0,6},{1,7},{2,4},{3,5},{4,2},{5,3},{6,0},{7,1},{8,14},{9,15},{10,... | collective-permute-start | bytes 393224 | tf_op jit(solution)/shard_map/exchange_tokens/ppermute | solution.py:276
  20.9 5.8 %collective-permute-start.4 = (f32[256,128]{1,0:T(8,128)S(1)}, f32[256,128]{1,0:T(8,128)S(1)}, u32[]{:S(2)}, u32[]{:S(2)}) collective-permute-start(f32[256,128]{1,0:T(8,128)S(1)} %get-tuple-element.33), channel_id=1, source_target_pairs={{0,2},{1,3},{2,0},{3,1},{4,6},{5,7},{6,4},{7,5},{8,10},{9,11},{10,... | collective-permute-start | bytes 393224 | tf_op jit(solution)/shard_map/exchange_tokens/ppermute | solution.py:276
  20.9 10.9 %collective-permute-start.8 = (bf16[8,128,128]{2,1,0:T(8,128)(2,1)S(1)}, bf16[8,128,128]{2,1,0:T(8,128)(2,1)S(1)}, u32[]{:S(2)}, u32[]{:S(2)}) collective-permute-start(bf16[8,128,128]{2,1,0:T(8,128)(2,1)S(1)} %all-to-all-done.refs_4_), channel_id=1, source_target_pairs={{0,16},{8,24},{16,0},{24,8},{32,48},{40,56},{48,32},{56,40},{64,80... | collective-permute-start | bytes 786440 | tf_op jit(solution)/shard_map/gather_queries/ppermute | solution.py:283
  22.3 13.9 %collective-permute-start.10 = (bf16[8,128,128]{2,1,0:T(8,128)(2,1)S(1)}, bf16[8,128,128]{2,1,0:T(8,128)(2,1)S(1)}, u32[]{:S(2)}, u32[]{:S(2)}) collective-permute-start(bf16[8,128,128]{2,1,0:T(8,128)(2,1)S(1)} %all-to-all-done.refs_4_), channel_id=1, source_target_pairs={{0,24},{8,16},{16,8},{24,0},{32,56},{40,48},{48,40},{56,32},{64,88... | collective-permute-start | bytes 786440 | tf_op jit(solution)/shard_map/gather_queries/ppermute | solution.py:283
  24.4 12.1 %collective-permute-start.11 = (bf16[8,128,128]{2,1,0:T(8,128)(2,1)S(1)}, bf16[8,128,128]{2,1,0:T(8,128)(2,1)S(1)}, u32[]{:S(2)}, u32[]{:S(2)}) collective-permute-start(bf16[8,128,128]{2,1,0:T(8,128)(2,1)S(1)} %all-to-all-done.refs_4_), channel_id=1, source_target_pairs={{0,8},{8,0},{16,24},{24,16},{32,40},{40,32},{48,56},{56,48},{64,72... | collective-permute-start | bytes 786440 | tf_op jit(solution)/shard_map/gather_queries/ppermute | solution.py:283
  27.0 1.2 %collective-permute-start.5 = (f32[32,128]{1,0:T(8,128)S(1)}, f32[32,128]{1,0:T(8,128)S(1)}, u32[]{:S(2)}, u32[]{:S(2)}) collective-permute-start(f32[32,128]{1,0:T(8,128)S(1)} %outer.1.refs_0_), channel_id=1, source_target_pairs={{0,1},{1,0},{2,3},{3,2},{4,5},{5,4},{6,7},{7,6},{8,9},{9,8},{10,11... | collective-permute-start | bytes 49160 | tf_op jit(solution)/shard_map/exchange_grad/ppermute | solution.py:276
  28.3 5.5 %collective-permute-start.6 = (f32[32,128]{1,0:T(8,128)S(1)}, f32[32,128]{1,0:T(8,128)S(1)}, u32[]{:S(2)}, u32[]{:S(2)}) collective-permute-start(f32[32,128]{1,0:T(8,128)S(1)} %sum_parts.1.x_ref.refs_0_), channel_id=1, source_target_pairs={{0,6},{1,7},{2,4},{3,5},{4,2},{5,3},{6,0},{7,1},{8,14},{9,15},{10,... | collective-permute-start | bytes 49160 | tf_op jit(solution)/shard_map/exchange_grad/ppermute | solution.py:276
  31.0 5.2 %collective-permute-start.7 = (f32[32,128]{1,0:T(8,128)S(1)}, f32[32,128]{1,0:T(8,128)S(1)}, u32[]{:S(2)}, u32[]{:S(2)}) collective-permute-start(f32[32,128]{1,0:T(8,128)S(1)} %sum_parts.1.x_ref.refs_0_), channel_id=1, source_target_pairs={{0,4},{1,5},{2,6},{3,7},{4,0},{5,1},{6,2},{7,3},{8,12},{9,13},{10,... | collective-permute-start | bytes 49160 | tf_op jit(solution)/shard_map/exchange_grad/ppermute | solution.py:276
  31.8 4.4 %collective-permute-start.9 = (f32[32,128]{1,0:T(8,128)S(1)}, f32[32,128]{1,0:T(8,128)S(1)}, u32[]{:S(2)}, u32[]{:S(2)}) collective-permute-start(f32[32,128]{1,0:T(8,128)S(1)} %after.1), channel_id=1, source_target_pairs={{0,2},{1,3},{2,0},{3,1},{4,6},{5,7},{6,4},{7,5},{8,10},{9,11},{10,... | collective-permute-start | bytes 49160 | tf_op jit(solution)/shard_map/exchange_grad/ppermute | solution.py:276
